TPU v7x, 32 devices: a whole 2x2x4 slice. The times are simulated.
32 devices in a mesh: ctx: 8 (over z, x), ch: 4 (over y, core).
Axes of the slice: x: 2, y: 2, z: 4, core: 2. Of those that a mesh axis runs over, the one named last changes fastest.
Arguments:
- tokens: bfloat16 [4096, 8192], P('ctx'), may hold values from -6 to 6
- in_weight: bfloat16 [8192, 3, 4096], P('ctx', None, 'ch'), may hold values from -0.0625 to 0.0625
- short_taps: float32 [3, 3, 4096], P(None, None, 'ch'), may hold values from -3 to 3
- decay_rates: float32 [16, 4096], P(None, 'ch'), may hold values from 0 to 0.034, as said below
- residues: float32 [16, 4096], P(None, 'ch'), may hold values from -1.5 to 1.5
Outputs:
- mixed: bfloat16 [4096, 4096], P(('ctx', 'ch'))
Inputs may be any that keep to these rules, and one draw needn't show every extreme that they name: `decay_rates`: positive decay rates.
All inputs are finite; a program needn't handle non-finite values.
Results may differ from a plain program's by a relative error of at most 0.0063.
Values may be sent and summed in bfloat16 or wider, within the bound.
No kernel may reach another device: no remote copies, remote signals or barrier semaphores. Data moves between devices by JAX's collectives and lax.ppermute only.
A program may use at most 128 MiB of HBM per device.

v0:
```python
import functools

import jax
import jax.numpy as jnp
from jax import lax
from jax.experimental import pallas as pl
from jax.experimental.pallas import tpu as pltpu
from jax.sharding import Mesh
from jax.sharding import PartitionSpec as P


def conv_kernel(order, pick, *refs):
    parts = refs[:-11]
    taps, decay, scaled, state_in, halo_in, out, state, halo, ext, prod, modes = refs[-11:]
    rows, width = out.shape[1], out.shape[2]
    mode_count = decay.shape[0]
    tiles, _, lane = modes.shape
    i = pl.program_id(0)

    @pl.when(i == 0)
    def _():
        state[...] = state_in[...]
        halo[...] = halo_in[...]

    ext[0:8, :] = halo[...]
    for p, value in enumerate(parts):

        @pl.when(pick[i] == p)
        def _(value=value):
            ext[8 : 8 + rows, :] = value[0]

    halo[...] = ext[rows : rows + 8, :]

    def branch(i):
        cols = slice(i * width, (i + 1) * width)
        return (
            taps[0:1, cols] * ext[8 : 8 + rows, cols]
            + taps[1:2, cols] * ext[7 : 7 + rows, cols]
            + taps[2:3, cols] * ext[6 : 6 + rows, cols]
        )

    prod[...] = branch(1) * branch(2)
    halves = [slice(s, s + 8) for s in range(0, mode_count, 8)]
    decays = [decay[h, :] for h in halves]
    scales = [scaled[h, :] for h in halves]

    def step(t, states):
        entry = jnp.broadcast_to(prod[pl.ds(t, 1), :], (8, width))
        states = tuple(d * s + entry for d, s in zip(decays, states))
        total = scales[0] * states[0]
        for c, s in zip(scales[1:], states[1:]):
            total = total + c * s
        for i in range(tiles):
            modes[i, pl.ds(pl.multiple_of(t * 8, 8), 8), :] = total[:, i * lane : (i + 1) * lane]
        return states

    states = lax.fori_loop(0, rows, step, tuple(state[h, :] for h in halves), unroll=8)
    for h, s in zip(halves, states):
        state[h, :] = s
    gate = branch(0)
    for i in range(tiles):
        cols = slice(i * lane, (i + 1) * lane)
        conv = modes[i, pl.ds(0, rows, stride=8), :]
        for s in range(1, 8):
            conv = conv + modes[i, pl.ds(s, rows, stride=8), :]
        out[0, :, cols] = (gate[:, cols] * conv).astype(out.dtype)


def run_conv(order, pick, parts, rows, taps, decay, scaled, state, halo):
    blocks = order.shape[0]
    width3 = taps.shape[1]
    width = width3 // 3
    mode_count = decay.shape[0]
    lane = min(128, width)

    def whole(shape):
        return pl.BlockSpec(shape, lambda i, order, pick: (0,) * len(shape))

    return pl.pallas_call(
        conv_kernel,
        out_shape=(
            jax.ShapeDtypeStruct((blocks, rows, width), jnp.bfloat16),
            jax.ShapeDtypeStruct((mode_count, width), jnp.float32),
            jax.ShapeDtypeStruct((8, width3), jnp.float32),
        ),
        grid_spec=pltpu.PrefetchScalarGridSpec(
            num_scalar_prefetch=2,
            grid=(blocks,),
            in_specs=[pl.BlockSpec((1, rows, width3), lambda i, order, pick: (order[i], 0, 0))] * len(parts)
            + [
                whole((3, width3)),
                whole((mode_count, width)),
                whole((mode_count, width)),
                whole((mode_count, width)),
                whole((8, width3)),
            ],
            out_specs=[
                pl.BlockSpec((1, rows, width), lambda i, order, pick: (i, 0, 0)),
                whole((mode_count, width)),
                whole((8, width3)),
            ],
            scratch_shapes=[
                pltpu.VMEM((rows + 8, width3), jnp.float32),
                pltpu.VMEM((rows, width), jnp.float32),
                pltpu.VMEM((width // lane, rows * 8, lane), jnp.float32),
            ],
        ),
        compiler_params=pltpu.CompilerParams(vmem_limit_bytes=24 * 1024 * 1024),
        cost_estimate=pl.CostEstimate(flops=0, bytes_accessed=0, transcendentals=0),
        name="conv",
    )(order, pick, *(p.reshape(-1, rows, width3) for p in parts), taps, decay, scaled, state, halo)


def cut_tokens_kernel(index, *refs):
    for i, source in enumerate(refs[:-1]):
        refs[-1][i] = source[...]


def cut_tokens(tokens, row_block, planes, rows):
    depth = tokens.shape[1] // planes

    def cut(i):
        return pl.BlockSpec((rows, depth), lambda n, index: (index[0], i))

    return pl.pallas_call(
        cut_tokens_kernel,
        out_shape=jax.ShapeDtypeStruct((planes, rows, depth), tokens.dtype),
        grid_spec=pltpu.PrefetchScalarGridSpec(
            num_scalar_prefetch=1,
            grid=(1,),
            in_specs=[cut(i) for i in range(planes)],
            out_specs=pl.BlockSpec((planes, rows, depth), lambda n, index: (0, 0, 0)),
        ),
        compiler_params=pltpu.CompilerParams(vmem_limit_bytes=48 * 1024 * 1024),
        cost_estimate=pl.CostEstimate(flops=0, bytes_accessed=0, transcendentals=0),
        name="cut_tokens",
    )(jnp.reshape(row_block, (1,)).astype(jnp.int32), *([tokens] * planes))


def cut_weight_kernel(index, *refs):
    width = refs[0].shape[2]
    for i, source in enumerate(refs[:-1]):
        refs[-1][:, i * width : (i + 1) * width] = source[0]


def cut_weight(weight, column_block, width, first_branch=0, branches=3):
    rows = weight.shape[1]
    if width % 128:
        cut = lax.dynamic_slice(weight, (first_branch, 0, column_block * width), (branches, rows, width))
        return jnp.transpose(cut, (1, 0, 2)).reshape(rows, branches * width)

    def cut(i):
        return pl.BlockSpec((1, rows, width), lambda n, index: (first_branch + i, 0, index[0]))

    return pl.pallas_call(
        cut_weight_kernel,
        out_shape=jax.ShapeDtypeStruct((rows, branches * width), weight.dtype),
        grid_spec=pltpu.PrefetchScalarGridSpec(
            num_scalar_prefetch=1,
            grid=(1,),
            in_specs=[cut(i) for i in range(branches)],
            out_specs=pl.BlockSpec((rows, branches * width), lambda n, index: (0, 0)),
        ),
        compiler_params=pltpu.CompilerParams(vmem_limit_bytes=48 * 1024 * 1024),
        cost_estimate=pl.CostEstimate(flops=0, bytes_accessed=0, transcendentals=0),
        name="cut_weight",
    )(jnp.reshape(column_block, (1,)).astype(jnp.int32), *([weight] * branches))


def chain_kernel(slots, planes, has_got, place, *refs):
    terms, refs = refs[: len(slots)], refs[len(slots) :]
    got, refs = (refs[0], refs[1:]) if has_got else (None, refs)
    held, sem = refs[-2:]
    total = refs[-3] if slots[-1] == planes - 1 else None
    sent = refs[-4 if total is not None else -3] if slots[0] < planes - 1 else None
    for slot, term in zip(slots, terms):

        @pl.when(place[0] == slot)
        def _(slot=slot, term=term):
            copy = pltpu.make_async_copy(term, held, sem)
            copy.start()
            copy.wait()
            value = held[...]
            if has_got:
                value = value + got[...].astype(jnp.float32)
            if slot == planes - 1:
                total[...] = value
            else:
                sent[...] = value.astype(sent.dtype)


def run_chain(place, slots, planes, terms, got, total):
    rows, width3 = terms[0].shape
    outs, aliases = [], {}
    inputs = [place, *terms] + ([got] if got is not None else [])
    if slots[0] < planes - 1:
        outs.append(jax.ShapeDtypeStruct((rows, width3), jnp.bfloat16))
    if slots[-1] == planes - 1:
        if total is not None:
            aliases = {len(inputs): len(outs)}
            inputs.append(total)
        outs.append(jax.ShapeDtypeStruct((rows, width3), jnp.float32))
    vmem = pl.BlockSpec(memory_space=pltpu.VMEM)
    specs = [pl.BlockSpec(memory_space=pltpu.SMEM)] + [pl.BlockSpec(memory_space=pl.ANY)] * len(terms)
    result = pl.pallas_call(
        functools.partial(chain_kernel, tuple(slots), planes, got is not None),
        out_shape=outs,
        in_specs=specs + [vmem] * (len(inputs) - len(specs)),
        out_specs=[vmem] * len(outs),
        scratch_shapes=[pltpu.VMEM((rows, width3), jnp.float32), pltpu.SemaphoreType.DMA],
        input_output_aliases=aliases,
        compiler_params=pltpu.CompilerParams(vmem_limit_bytes=16 * 1024 * 1024),
        cost_estimate=pl.CostEstimate(flops=0, bytes_accessed=0, transcendentals=0),
        name="chain",
    )(*inputs)
    sent = result[0] if slots[0] < planes - 1 else None
    return sent, (result[-1] if slots[-1] == planes - 1 else None)


def term_kernel(*refs):
    blocks, weight, out = refs[:-2], refs[-2], refs[-1]
    row = 0
    for block in blocks:
        rows = block.shape[0]
        out[row : row + rows, :] = jnp.dot(block[...], weight[...], preferred_element_type=jnp.float32)
        row += rows


def term(blocks, weight):
    depth, width = weight.shape
    rows = sum(b.shape[0] for b in blocks)
    step = width // 3 if width // 3 % 128 == 0 else width
    return pl.pallas_call(
        term_kernel,
        out_shape=jax.ShapeDtypeStruct((rows, width), jnp.float32),
        grid=(width // step,),
        in_specs=[pl.BlockSpec(b.shape, lambda n: (0, 0)) for b in blocks]
        + [pl.BlockSpec((depth, step), lambda n: (0, n))],
        out_specs=pl.BlockSpec((rows, step), lambda n: (0, n)),
        compiler_params=pltpu.CompilerParams(vmem_limit_bytes=32 * 1024 * 1024),
        cost_estimate=pl.CostEstimate(flops=0, bytes_accessed=0, transcendentals=0),
        name="term",
    )(*blocks, weight)


def join_kernel(first, second, out):
    half = first.shape[2]
    out[:, :half] = first[0]
    out[:, half:] = second[0]


def join(first, second, order):
    blocks, rows, half = first.shape
    if half % 128:
        both = jnp.stack([first, second]).reshape((2,) + order + (rows, half))
        return both.transpose(4, 2, 3, 1, 0, 5).reshape(rows, -1)
    xs, ys, cs = order

    def source(i):
        return (i % xs) * ys * cs + i // xs

    return pl.pallas_call(
        join_kernel,
        out_shape=jax.ShapeDtypeStruct((rows, 2 * blocks * half), first.dtype),
        grid=(blocks,),
        in_specs=[pl.BlockSpec((1, rows, half), lambda i: (source(i), 0, 0))] * 2,
        out_specs=pl.BlockSpec((rows, 2 * half), lambda i: (0, i)),
        compiler_params=pltpu.CompilerParams(vmem_limit_bytes=8 * 1024 * 1024),
        name="join",
    )(first, second)


def after(value, *others):
    return lax.optimization_barrier((value, *others))[0]


def ring(axis, k):
    count = lax.axis_size(axis)
    return [(s, (s + k) % count) for s in range(count)]


def gather_rel(value, axis):
    count = lax.axis_size(axis)
    pieces = [value] + [lax.ppermute(value, axis, ring(axis, k)) for k in range(1, count)]
    return jnp.concatenate(pieces, axis=0) if count > 1 else value


def shards(tokens, in_weight, short_taps, decay_rates, residues):
    Z, X, Y, C = (lax.axis_size(a) for a in ("z", "x", "y", "c"))
    z, x, y, c = (lax.axis_index(a) for a in ("z", "x", "y", "c"))
    tok_rows, depth = tokens.shape
    w_rows, _, chans = in_weight.shape
    own = chans // X
    half = own // 2
    plane_depth = X * w_rows

    lower = z < Z // 2
    far_block = jnp.where(lower, 0, 1)
    near_block = 1 - far_block

    weight = jnp.transpose(in_weight, (1, 0, 2))

    def sends(block, *branches):
        return [cut_weight(weight, 2 * ((x + k) % X) + block, half, *branches) for k in range(1, X)]

    def moved(pieces):
        return [lax.ppermute(p, "x", ring("x", k + 1)) for k, p in enumerate(pieces)]

    def assemble(kept, pieces):
        held = [kept] + pieces
        rows = []
        for i in range(X):
            row = held[0]
            for k in range(1, X):
                row = jnp.where((x - i) % X == k, held[k], row)
            rows.append(row)
        return jnp.concatenate(rows, axis=0)

    share = tok_rows // (Y * C)
    far_sends = sends(far_block)
    far_got = moved(far_sends)
    mine = cut_tokens(after(tokens, *far_sends), y * C + c, Z, share)
    split = lax.all_to_all(mine, "z", split_axis=0, concat_axis=0, tiled=True)
    near_sends = [sends(near_block, 0, 1), sends(near_block, 1, 2)]
    near_got = [moved([after(p, *far_got) for p in near_sends[0]]), None]
    kept = [cut_weight(weight, 2 * x + block, half) for block in (far_block, near_block)]
    split = list(after(split, *near_got[0], *near_sends[1], *kept))
    far_weight = assemble(kept[0], far_got)
    near_weight = None

    pairs, others = [], []
    sent_ups = []

    def first_step(k, *before):
        pairs.append(gather_rel(after(split[k], *before), "xy"[k % 2]))

    def second_step(k, *before):
        axis = "yx"[k % 2]
        value = after(pairs[k], *before)
        others.append([lax.ppermute(value, axis, ring(axis, j)) for j in range(1, lax.axis_size(axis))])

    def add_planes(k):
        planes = range(k, min(k + 2, Z))
        for i in planes:
            first_step(i, *sent_ups[max(0, k - 2) : k - 1])
        for i in planes:
            second_step(i, *(sent_ups[k - 1 + i % 2 : k + i % 2] if k else []))

    def places(*sizes):
        grids = jnp.meshgrid(*(jnp.arange(n, dtype=jnp.int32) for n in sizes), indexing="ij")
        return [g.reshape(-1) for g in grids]

    bx, by, bc = places(X, Y, C)
    rel_x, rel_y, rel_c = (x - bx) % X, (y - by) % Y, (c - bc) % C
    group_rows = X * Y * C * share
    lead = [C * (X, Y)[k % 2] * share for k in range(Z)]

    def rows_of(k):
        column, inner = (rel_y, rel_x) if k % 2 == 0 else (rel_x, rel_y)
        head, tail = k * group_rows, k * group_rows + lead[k]
        if k < 2:
            head, tail = (0, lead[0] + lead[1]) if k == 0 else (lead[0], group_rows + lead[1])
        place = jnp.where(column == 0, head, tail + (column - 1) * lead[k])
        return place + rel_c * (lead[k] // C) + inner * share

    def near_cut(value):
        return lax.dynamic_slice_in_dim(value, x * own + near_block * half, half, axis=value.ndim - 1)

    taps = near_cut(short_taps).reshape(3, 3 * half)
    decay = near_cut(jnp.exp(-decay_rates))
    scaled = near_cut(residues * jnp.sqrt(2.0 * decay_rates))

    unit_rows = group_rows * Z // 8
    count = group_rows * Z // unit_rows
    place_up = jnp.reshape(z, (1,)).astype(jnp.int32)
    place_down = Z - 1 - place_up
    far, near = {}, {}
    ups, downs = {}, {}
    totals = []
    state = jnp.zeros_like(decay)
    halo = jnp.zeros((8, 3 * half), jnp.float32)
    outs = []
    before = []
    came, due = {}, {}

    blocks, columns, used = [], [], list(range(Z))
    add_planes(0)

    def unit(u):
        nonlocal blocks
        rows, have = [], 0
        while have < unit_rows:
            if not blocks:
                if not columns:
                    k = used.pop(0)
                    while len(pairs) <= k:
                        add_planes(len(pairs))
                    if k == 0:
                        columns.extend(pairs[:2] + others[0] + others[1])
                        used.pop(0)
                    else:
                        columns.extend([pairs[k]] + others[k])
                value = columns.pop(0)
                blocks = [value]
                if u > 0:
                    value = after(value, sent_ups[max(0, u - 2)])
                blocks += [lax.ppermute(value, "c", ring("c", j)) for j in range(1, C)]
            block = blocks.pop(0)
            if block.shape[0] > unit_rows - have:
                blocks.insert(0, block[unit_rows - have :])
                block = block[: unit_rows - have]
            rows.append(block)
            have += block.shape[0]
        rows[0] = after(rows[0], *sent_ups[u - 1 : u])
        return rows

    def ready(plane):
        return group_rows + lead[1] if plane == 0 else (plane + 1) * group_rows

    def emit(plane):
        nonlocal state, halo
        first = 0 if plane < 2 else plane * group_rows
        begin, end = first // unit_rows, -(-ready(plane) // unit_rows)
        rows = rows_of(plane) - begin * unit_rows
        out, state, halo = run_conv(
            rows % unit_rows // share, rows // unit_rows, totals[begin:end], share, taps, decay, scaled, state, halo
        )
        outs.append(out.reshape(X * Y * C, share, half))
        return out

    for tick in range(count + 2 * (Z - 1)):
        slots = [s for s in range(Z) if 0 <= tick - 2 * s < count]
        if tick < count:
            value = unit(tick)
            far[tick] = term(value, far_weight)
            near[tick] = value
        u = tick - 2 * (Z // 2)
        if 0 <= u < count:
            if near_weight is None:
                near_got[1] = moved([after(p, *sent_ups[1:2]) for p in near_sends[1]])
                whole = [jnp.concatenate(p, axis=1) for p in zip(*near_got)]
                near_weight = assemble(kept[1], [after(p, *sent_ups[tick - 1 : tick]) for p in whole])
            value = after(near[u][0], *(sent_ups[tick - 1 : tick] or before))
            near[u] = term([value] + near[u][1:], near_weight)
        terms = [(far if s < Z // 2 else near)[tick - 2 * s] for s in slots]
        sent_up, total = run_chain(after(place_up, *before), slots, Z, terms, ups.get(tick - 2), None)
        if sent_up is not None:
            ups[tick] = lax.ppermute(sent_up, "z", [(s, s + 1) for s in slots if s + 1 < Z])
            sent_ups.append(sent_up)
        before = [total if sent_up is None else sent_up]
        sent_down, total = run_chain(after(place_down, *before), slots, Z, terms, downs.get(tick - 2), total)
        if sent_down is not None:
            downs[tick] = lax.ppermute(sent_down, "z", [(Z - 1 - s, Z - 2 - s) for s in slots if s + 1 < Z])
        before = [total if sent_down is None else sent_down] + due.pop(tick + 1, [])
        if total is not None:
            totals.append(total)
            if len(outs) < Z and len(totals) * unit_rows >= ready(len(outs)):
                k = len(outs)
                before.append(emit(k))
                for home in (0, Z - 1):
                    if 0 < abs(k - home) < Z - 1 and tick + 3 < count + 2 * (Z - 1):
                        came[home, k] = lax.ppermute(outs[k], "z", [(home, k)])
                        due.setdefault(count + 2 * (Z - 1) - 1, []).append(came[home, k])
    while len(outs) < Z:
        emit(len(outs))

    def collect(home):
        total = jnp.where(z == home, outs[home], jnp.zeros_like(outs[home]))
        for k in range(Z):
            if k != home:
                if (home, k) not in came:
                    value = after(outs[k], totals[-1]) if k == 0 else outs[k]
                    came[home, k] = lax.ppermute(value, "z", [(home, k)])
                total = total + came[home, k]
        return total

    def spread(total):
        return lax.all_to_all(total, ("x", "y", "c"), split_axis=0, concat_axis=0, tiled=True)

    return join(spread(collect(Z - 1)), spread(collect(0)), (X, Y, C))


def solution(mesh):
    ctx, ch = mesh.shape["ctx"], mesh.shape["ch"]
    xs = 1
    while 4 * xs * xs <= ctx:
        xs *= 2
    cs = 2 if ch % 2 == 0 else 1
    fine = Mesh(mesh.devices.reshape(ctx // xs, xs, ch // cs, cs), ("z", "x", "y", "c"))
    return jax.shard_map(
        shards,
        mesh=fine,
        in_specs=(
            P(("z", "x"), None),
            P(("z", "x"), None, ("y", "c")),
            P(None, None, ("y", "c")),
            P(None, ("y", "c")),
            P(None, ("y", "c")),
        ),
        out_specs=P(("z", "x", "y", "c"), None),
        check_vma=False,
    )
```

profile of v0, /device:TPU:0, one launch (start us, length us, event | category | flops | bytes accessed | tf_op | source)
XLA Modules:
  0.0 366.0 jit_solution(11377741566808407772)
XLA Ops:
  4.5 6.3 %all-to-all-start = ((bf16[4,128,2048]{2,1,0:T(8,128)(2,1)}), bf16[4,128,2048]{2,1,0:T(8,128)(2,1)}, u32[]{:S(2)}, u32[]{:S(2)}) async-start(bf16[4,128,2048]{2,1,0:T(8,128)(2,1)} %cut_tokens.1), calls=%async_computation | async-start | bytes 4194304 | tf_op jit(solution)/shard_map/all_to_all | solution.py:323
  13.4 33.4 %collective-permute-done = bf16[1024,768]{1,0:T(8,128)(2,1)} collective-permute-done((bf16[1024,768]{1,0:T(8,128)(2,1)S(1)}, bf16[1024,768]{1,0:T(8,128)(2,1)}, u32[]{:S(2)}, u32[]{:S(2)}) %collective-permute-start) | collective-permute-done | bytes 1572896 | tf_op jit(solution)/shard_map/ppermute | solution.py:307
  65.1 9.6 %collective-permute-done.2 = bf16[128,2048]{1,0:T(8,128)(2,1)S(1)} collective-permute-done((bf16[128,2048]{1,0:T(8,128)(2,1)S(1)}, bf16[128,2048]{1,0:T(8,128)(2,1)S(1)}, u32[]{:S(2)}, u32[]{:S(2)}) %collective-permute-start.2) | collective-permute-done | bytes 524320 | tf_op jit(solution)/shard_map/ppermute | solution.py:284
  90.0 14.7 %collective-permute-done.10.refs_0_ = bf16[256,2048]{1,0:T(8,128)(2,1)S(1)} collective-permute-done((bf16[256,2048]{1,0:T(8,128)(2,1)S(1)}, bf16[256,2048]{1,0:T(8,128)(2,1)S(1)}, u32[]{:S(2)}, u32[]{:S(2)}) %collective-permute-start.10) | collective-permute-done | bytes 1048608 | tf_op jit(solution)/shard_map/ppermute | solution.py:340
  109.7 5.4 %collective-permute-done.14 = bf16[128,2048]{1,0:T(8,128)(2,1)S(1)} collective-permute-done((bf16[128,2048]{1,0:T(8,128)(2,1)S(1)}, bf16[128,2048]{1,0:T(8,128)(2,1)S(1)}, u32[]{:S(2)}, u32[]{:S(2)}) %collective-permute-start.14) | collective-permute-done | bytes 524320 | tf_op jit(solution)/shard_map/ppermute | solution.py:284
  129.4 7.9 %collective-permute-done.12.refs_2_ = bf16[512,768]{1,0:T(8,128)(2,1)S(1)} collective-permute-done((bf16[512,768]{1,0:T(8,128)(2,1)S(1)}, bf16[512,768]{1,0:T(8,128)(2,1)S(1)}, u32[]{:S(2)}, u32[]{:S(2)}) %collective-permute-start.12) | collective-permute-done | bytes 786464 | tf_op jit(solution)/shard_map/ppermute | solution.py:448
  152.9 6.8 %collective-permute-done.17.refs_3_ = bf16[512,768]{1,0:T(8,128)(2,1)S(1)} collective-permute-done((bf16[512,768]{1,0:T(8,128)(2,1)S(1)}, bf16[512,768]{1,0:T(8,128)(2,1)S(1)}, u32[]{:S(2)}, u32[]{:S(2)}) %collective-permute-start.17) | collective-permute-done | bytes 786464 | tf_op jit(solution)/shard_map/ppermute | solution.py:448
  160.8 5.0 %collective-permute-start.25 = (bf16[512,768]{1,0:T(8,128)(2,1)S(1)}, bf16[512,768]{1,0:T(8,128)(2,1)S(1)}, u32[]{:S(2)}, u32[]{:S(2)}) collective-permute-start(bf16[512,768]{1,0:T(8,128)(2,1)S(1)} %chain.36), channel_id=1, source_target_pairs={{0,8},{8,16},{16,24},{1,9},{9,17},{17,25},{2,10},{10,18},{18,26},{... | collective-permute-start | bytes 2359304 | tf_op jit(solution)/shard_map/ppermute | solution.py:448
  171.9 4.6 %collective-permute-done.21.refs_3_ = bf16[512,768]{1,0:T(8,128)(2,1)S(1)} collective-permute-done((bf16[512,768]{1,0:T(8,128)(2,1)S(1)}, bf16[512,768]{1,0:T(8,128)(2,1)S(1)}, u32[]{:S(2)}, u32[]{:S(2)}) %collective-permute-start.21) | collective-permute-done | bytes 786464 | tf_op jit(solution)/shard_map/ppermute | solution.py:448
  179.1 8.0 %collective-permute-start.29 = (bf16[512,768]{1,0:T(8,128)(2,1)}, bf16[512,768]{1,0:T(8,128)(2,1)}, u32[]{:S(2)}, u32[]{:S(2)}) collective-permute-start(bf16[512,768]{1,0:T(8,128)(2,1)} %chain.38), channel_id=1, source_target_pairs={{0,8},{8,16},{16,24},{1,9},{9,17},{17,25},{2,10},{10,18},{18,26},{... | collective-permute-start | bytes 2359304 | tf_op jit(solution)/shard_map/ppermute | solution.py:448
  197.0 5.5 %collective-permute-start.31 = (bf16[512,768]{1,0:T(8,128)(2,1)}, bf16[512,768]{1,0:T(8,128)(2,1)}, u32[]{:S(2)}, u32[]{:S(2)}) collective-permute-start(bf16[512,768]{1,0:T(8,128)(2,1)} %get-tuple-element.131), channel_id=1, source_target_pairs={{0,8},{8,16},{16,24},{1,9},{9,17},{17,25},{2,10},{10,18},{18,26},{... | collective-permute-start | bytes 2359304 | tf_op jit(solution)/shard_map/ppermute | solution.py:448
  222.0 4.6 %collective-permute-start.33 = (bf16[512,768]{1,0:T(8,128)(2,1)S(1)}, bf16[512,768]{1,0:T(8,128)(2,1)S(1)}, u32[]{:S(2)}, u32[]{:S(2)}) collective-permute-start(bf16[512,768]{1,0:T(8,128)(2,1)S(1)} %get-tuple-element.140), channel_id=1, source_target_pairs={{0,8},{8,16},{16,24},{1,9},{9,17},{17,25},{2,10},{10,18},{18,26},{... | collective-permute-start | bytes 2359304 | tf_op jit(solution)/shard_map/ppermute | solution.py:448
  236.7 6.7 %conv.4 = (bf16[8,128,256]{2,1,0:T(8,128)(2,1)}, f32[16,256]{1,0:T(8,128)S(1)}, f32[8,768]{1,0:T(8,128)S(1)}) custom-call(s32[8]{0:T(128)S(1)} %get-tuple-element.215.order, s32[8]{0:T(128)S(1)} %get-tuple-element.212.pick, f32[4,128,768]{2,1,0:T(8,128)S(1)} %bitcast.30, f32[4,128,768]{2,1,0:T(8,128)S(1)} %bitcast.32, f32[4,128,768]{2,1,0:T(8,128)S(1)} %bitcast.26, ...), custom_call_target="tpu_custom_call" | custom-call | tf_op jit(solution)/shard_map/conv/pallas_call | solution.py:79
  246.6 5.2 %collective-permute-done.34.refs_3_ = bf16[512,768]{1,0:T(8,128)(2,1)S(1)} collective-permute-done((bf16[512,768]{1,0:T(8,128)(2,1)S(1)}, bf16[512,768]{1,0:T(8,128)(2,1)S(1)}, u32[]{:S(2)}, u32[]{:S(2)}) %collective-permute-start.34) | collective-permute-done | bytes 786464 | tf_op jit(solution)/shard_map/ppermute | solution.py:453
  253.4 6.1 %conv.5 = (bf16[8,128,256]{2,1,0:T(8,128)(2,1)S(1)}, f32[16,256]{1,0:T(8,128)S(1)}, f32[8,768]{1,0:T(8,128)S(1)}) custom-call(s32[8]{0:T(128)S(1)} %get-tuple-element.214.order, s32[8]{0:T(128)S(1)} %get-tuple-element.194.pick, f32[4,128,768]{2,1,0:T(8,128)S(1)} %bitcast.31, f32[4,128,768]{2,1,0:T(8,128)S(1)} %bitcast.33, f32[4,128,768]{2,1,0:T(8,128)S(1)} %bitcast.27, ...), custom_call_target="tpu_custom_call" | custom-call | tf_op jit(solution)/shard_map/conv/pallas_call | solution.py:79
  262.7 5.9 %collective-permute-done.36.refs_2_ = bf16[512,768]{1,0:T(8,128)(2,1)S(1)} collective-permute-done((bf16[512,768]{1,0:T(8,128)(2,1)S(1)}, bf16[512,768]{1,0:T(8,128)(2,1)S(1)}, u32[]{:S(2)}, u32[]{:S(2)}) %collective-permute-start.36) | collective-permute-done | bytes 786464 | tf_op jit(solution)/shard_map/ppermute | solution.py:453
  274.9 10.6 %collective-permute-done.38.refs_2_ = bf16[512,768]{1,0:T(8,128)(2,1)S(1)} collective-permute-done((bf16[512,768]{1,0:T(8,128)(2,1)S(1)}, bf16[512,768]{1,0:T(8,128)(2,1)S(1)}, u32[]{:S(2)}, u32[]{:S(2)}) %collective-permute-start.38) | collective-permute-done | bytes 786464 | tf_op jit(solution)/shard_map/ppermute | solution.py:453
  287.0 4.6 %collective-permute-start.41 = (bf16[8,128,256]{2,1,0:T(8,128)(2,1)S(1)}, bf16[8,128,256]{2,1,0:T(8,128)(2,1)S(1)}, u32[]{:S(2)}, u32[]{:S(2)}) collective-permute-start(bf16[8,128,256]{2,1,0:T(8,128)(2,1)S(1)} %get-tuple-element.163), channel_id=1, source_target_pairs={{0,8},{1,9},{2,10},{3,11},{4,12},{5,13},{6,14},{7,15}} | collective-permute-start | bytes 1572872 | tf_op jit(solution)/shard_map/ppermute | solution.py:462
  292.4 5.9 %conv.6 = (bf16[8,128,256]{2,1,0:T(8,128)(2,1)S(1)}, f32[16,256]{1,0:T(8,128)S(1)}, f32[8,768]{1,0:T(8,128)S(1)}) custom-call(s32[8]{0:T(128)S(1)} %and_select_fusion.1.order, s32[8]{0:T(128)S(1)} %get-tuple-element.210.pick, f32[4,128,768]{2,1,0:T(8,128)S(1)} %bitcast.35, f32[4,128,768]{2,1,0:T(8,128)S(1)} %bitcast.36, f32[3,768]{1,0:T(4,128)S(1)} %bitcast.39, ...), custom_call_target="tpu_custom_call" | custom-call | tf_op jit(solution)/shard_map/conv/pallas_call | solution.py:79
  304.0 14.6 %collective-permute-done.44.refs_1_ = bf16[512,768]{1,0:T(8,128)(2,1)S(1)} collective-permute-done((bf16[512,768]{1,0:T(8,128)(2,1)S(1)}, bf16[512,768]{1,0:T(8,128)(2,1)S(1)}, u32[]{:S(2)}, u32[]{:S(2)}) %collective-permute-start.44) | collective-permute-done | bytes 786464 | tf_op jit(solution)/shard_map/ppermute | solution.py:453
  318.8 6.4 %conv.7 = (bf16[8,128,256]{2,1,0:T(8,128)(2,1)S(1)}, f32[16,256]{1,0:T(8,128)}, f32[8,768]{1,0:T(8,128)}) custom-call(s32[8]{0:T(128)S(1)} %and_select_fusion.10.order, s32[8]{0:T(128)S(1)} %get-tuple-element.189.pick, f32[4,128,768]{2,1,0:T(8,128)S(1)} %bitcast.28, f32[4,128,768]{2,1,0:T(8,128)S(1)} %bitcast.29, f32[3,768]{1,0:T(4,128)S(1)} %bitcast.40, ...), custom_call_target="tpu_custom_call" | custom-call | tf_op jit(solution)/shard_map/conv/pallas_call | solution.py:79
  329.3 8.3 %collective-permute-done.48 = bf16[8,128,256]{2,1,0:T(8,128)(2,1)} collective-permute-done((bf16[8,128,256]{2,1,0:T(8,128)(2,1)S(1)}, bf16[8,128,256]{2,1,0:T(8,128)(2,1)}, u32[]{:S(2)}, u32[]{:S(2)}) %collective-permute-start.48) | collective-permute-done | bytes 524320 | tf_op jit(solution)/shard_map/ppermute | solution.py:473
  346.4 5.5 %all-to-all-done.2.second = bf16[8,128,256]{2,1,0:T(8,128)(2,1)S(1)} async-done(((bf16[8,128,256]{2,1,0:T(8,128)(2,1)}), bf16[8,128,256]{2,1,0:T(8,128)(2,1)S(1)}, u32[]{:S(2)}, u32[]{:S(2)}) %all-to-all-start.2) | async-done | bytes 524320 | tf_op jit(solution)/shard_map/all_to_all | solution.py:478
  351.9 11.4 %all_to_all.15.first = bf16[8,128,256]{2,1,0:T(8,128)(2,1)S(1)} all-to-all(bf16[8,128,256]{2,1,0:T(8,128)(2,1)S(1)} %add_add_fusion.1), channel_id=1, replica_groups=mesh['z'=4,'x'=2,'y'=2,'c'=2] {'x','y','c'}, dimensions={0} | all-to-all | bytes 1048576 | tf_op jit(solution)/shard_map/all_to_all | solution.py:478
  (254 shorter events, 161.4 us)
Async XLA Ops:
  4.5 54.8 %all-to-all-start = ((bf16[4,128,2048]{2,1,0:T(8,128)(2,1)}), bf16[4,128,2048]{2,1,0:T(8,128)(2,1)}, u32[]{:S(2)}, u32[]{:S(2)}) async-start(bf16[4,128,2048]{2,1,0:T(8,128)(2,1)} %cut_tokens.1), calls=%async_computation | async-start | bytes 4194304 | tf_op jit(solution)/shard_map/all_to_all | solution.py:323
  10.8 36.0 %collective-permute-start = (bf16[1024,768]{1,0:T(8,128)(2,1)S(1)}, bf16[1024,768]{1,0:T(8,128)(2,1)}, u32[]{:S(2)}, u32[]{:S(2)}) collective-permute-start(bf16[1024,768]{1,0:T(8,128)(2,1)S(1)} %cut_weight.5), channel_id=1, source_target_pairs={{0,4},{4,0},{1,5},{5,1},{2,6},{6,2},{3,7},{7,3},{8,12},{12,8},{9,1... | collective-permute-start | bytes 4718600 | tf_op jit(solution)/shard_map/ppermute | solution.py:307
  78.6 26.1 %collective-permute-start.10 = (bf16[256,2048]{1,0:T(8,128)(2,1)S(1)}, bf16[256,2048]{1,0:T(8,128)(2,1)S(1)}, u32[]{:S(2)}, u32[]{:S(2)}) collective-permute-start(bf16[256,2048]{1,0:T(8,128)(2,1)S(1)} %pad_maximum_fusion.4.refs_0_), channel_id=1, source_target_pairs={{0,4},{4,0},{1,5},{5,1},{2,6},{6,2},{3,7},{7,3},{8,12},{12,8},{9,1... | collective-permute-start | bytes 3145736 | tf_op jit(solution)/shard_map/ppermute | solution.py:340
  80.1 26.1 %collective-permute-start.6 = (bf16[256,2048]{1,0:T(8,128)(2,1)S(1)}, bf16[256,2048]{1,0:T(8,128)(2,1)S(1)}, u32[]{:S(2)}, u32[]{:S(2)}) collective-permute-start(bf16[256,2048]{1,0:T(8,128)(2,1)S(1)} %pad_maximum_fusion.3.refs_0_), channel_id=1, source_target_pairs={{0,2},{2,0},{1,3},{3,1},{4,6},{6,4},{5,7},{7,5},{8,10},{10,8},{9,1... | collective-permute-start | bytes 3145736 | tf_op jit(solution)/shard_map/ppermute | solution.py:340
  87.3 27.8 %collective-permute-start.14 = (bf16[128,2048]{1,0:T(8,128)(2,1)S(1)}, bf16[128,2048]{1,0:T(8,128)(2,1)S(1)}, u32[]{:S(2)}, u32[]{:S(2)}) collective-permute-start(bf16[128,2048]{1,0:T(8,128)(2,1)S(1)} %copy-done.42), channel_id=1, source_target_pairs={{0,4},{4,0},{1,5},{5,1},{2,6},{6,2},{3,7},{7,3},{8,12},{12,8},{9,1... | collective-permute-start | bytes 1572872 | tf_op jit(solution)/shard_map/ppermute | solution.py:284
  87.9 30.8 %collective-permute-start.8 = (bf16[512,768]{1,0:T(8,128)(2,1)S(1)}, bf16[512,768]{1,0:T(8,128)(2,1)S(1)}, u32[]{:S(2)}, u32[]{:S(2)}) collective-permute-start(bf16[512,768]{1,0:T(8,128)(2,1)S(1)} %chain.28), channel_id=1, source_target_pairs={{0,8},{1,9},{2,10},{3,11},{4,12},{5,13},{6,14},{7,15}} | collective-permute-start | bytes 2359304 | tf_op jit(solution)/shard_map/ppermute | solution.py:448
  143.2 34.5 %collective-permute-start.27 = (bf16[256,2048]{1,0:T(8,128)(2,1)S(1)}, bf16[256,2048]{1,0:T(8,128)(2,1)}, u32[]{:S(2)}, u32[]{:S(2)}) collective-permute-start(bf16[256,2048]{1,0:T(8,128)(2,1)S(1)} %constant_dynamic-update-slice_fusion.2.refs_0_), channel_id=1, source_target_pairs={{0,4},{4,0},{1,5},{5,1},{2,6},{6,2},{3,7},{7,3},{8,12},{12,8},{9,1... | collective-permute-start | bytes 3145736 | tf_op jit(solution)/shard_map/ppermute | solution.py:340
  144.1 32.5 %collective-permute-start.21 = (bf16[512,768]{1,0:T(8,128)(2,1)S(1)}, bf16[512,768]{1,0:T(8,128)(2,1)S(1)}, u32[]{:S(2)}, u32[]{:S(2)}) collective-permute-start(bf16[512,768]{1,0:T(8,128)(2,1)S(1)} %chain.34), channel_id=1, source_target_pairs={{0,8},{8,16},{1,9},{9,17},{2,10},{10,18},{3,11},{11,19},{4,12},{12... | collective-permute-start | bytes 2359304 | tf_op jit(solution)/shard_map/ppermute | solution.py:448
  160.0 28.1 %collective-permute-start.24 = (bf16[256,2048]{1,0:T(8,128)(2,1)S(1)}, bf16[256,2048]{1,0:T(8,128)(2,1)S(1)}, u32[]{:S(2)}, u32[]{:S(2)}) collective-permute-start(bf16[256,2048]{1,0:T(8,128)(2,1)S(1)} %constant_dynamic-update-slice_fusion.2.refs_0_), channel_id=1, source_target_pairs={{0,1},{1,0},{2,3},{3,2},{4,5},{5,4},{6,7},{7,6},{8,9},{9,8},{10,11... | collective-permute-start | bytes 3145736 | tf_op jit(solution)/shard_map/ppermute | solution.py:407
  160.8 33.6 %collective-permute-start.25 = (bf16[512,768]{1,0:T(8,128)(2,1)S(1)}, bf16[512,768]{1,0:T(8,128)(2,1)S(1)}, u32[]{:S(2)}, u32[]{:S(2)}) collective-permute-start(bf16[512,768]{1,0:T(8,128)(2,1)S(1)} %chain.36), channel_id=1, source_target_pairs={{0,8},{8,16},{16,24},{1,9},{9,17},{17,25},{2,10},{10,18},{18,26},{... | collective-permute-start | bytes 2359304 | tf_op jit(solution)/shard_map/ppermute | solution.py:448
  177.7 38.6 %collective-permute-start.28 = (bf16[256,2048]{1,0:T(8,128)(2,1)}, bf16[256,2048]{1,0:T(8,128)(2,1)}, u32[]{:S(2)}, u32[]{:S(2)}) collective-permute-start(bf16[256,2048]{1,0:T(8,128)(2,1)} %collective-permute-done.27.refs_0_), channel_id=1, source_target_pairs={{0,1},{1,0},{2,3},{3,2},{4,5},{5,4},{6,7},{7,6},{8,9},{9,8},{10,11... | collective-permute-start | bytes 3145736 | tf_op jit(solution)/shard_map/ppermute | solution.py:407
  177.8 25.0 %collective-permute-start.26 = (bf16[512,768]{1,0:T(8,128)(2,1)}, bf16[512,768]{1,0:T(8,128)(2,1)}, u32[]{:S(2)}, u32[]{:S(2)}) collective-permute-start(bf16[512,768]{1,0:T(8,128)(2,1)} %chain.37), channel_id=1, source_target_pairs={{24,16},{16,8},{8,0},{25,17},{17,9},{9,1},{26,18},{18,10},{10,2},{... | collective-permute-start | bytes 2359304 | tf_op jit(solution)/shard_map/ppermute | solution.py:453
  179.1 41.4 %collective-permute-start.29 = (bf16[512,768]{1,0:T(8,128)(2,1)}, bf16[512,768]{1,0:T(8,128)(2,1)}, u32[]{:S(2)}, u32[]{:S(2)}) collective-permute-start(bf16[512,768]{1,0:T(8,128)(2,1)} %chain.38), channel_id=1, source_target_pairs={{0,8},{8,16},{16,24},{1,9},{9,17},{17,25},{2,10},{10,18},{18,26},{... | collective-permute-start | bytes 2359304 | tf_op jit(solution)/shard_map/ppermute | solution.py:448
  188.1 38.5 %collective-permute-start.30 = (bf16[512,768]{1,0:T(8,128)(2,1)}, bf16[512,768]{1,0:T(8,128)(2,1)}, u32[]{:S(2)}, u32[]{:S(2)}) collective-permute-start(bf16[512,768]{1,0:T(8,128)(2,1)} %chain.39), channel_id=1, source_target_pairs={{24,16},{16,8},{8,0},{25,17},{17,9},{9,1},{26,18},{18,10},{10,2},{... | collective-permute-start | bytes 2359304 | tf_op jit(solution)/shard_map/ppermute | solution.py:453
  197.0 35.0 %collective-permute-start.31 = (bf16[512,768]{1,0:T(8,128)(2,1)}, bf16[512,768]{1,0:T(8,128)(2,1)}, u32[]{:S(2)}, u32[]{:S(2)}) collective-permute-start(bf16[512,768]{1,0:T(8,128)(2,1)} %get-tuple-element.131), channel_id=1, source_target_pairs={{0,8},{8,16},{16,24},{1,9},{9,17},{17,25},{2,10},{10,18},{18,26},{... | collective-permute-start | bytes 2359304 | tf_op jit(solution)/shard_map/ppermute | solution.py:448
  233.1 28.8 %collective-permute-start.35 = (bf16[512,768]{1,0:T(8,128)(2,1)S(1)}, bf16[512,768]{1,0:T(8,128)(2,1)S(1)}, u32[]{:S(2)}, u32[]{:S(2)}) collective-permute-start(bf16[512,768]{1,0:T(8,128)(2,1)S(1)} %get-tuple-element.146), channel_id=1, source_target_pairs={{8,16},{16,24},{9,17},{17,25},{10,18},{18,26},{11,19},{19,27},{12,... | collective-permute-start | bytes 2359304 | tf_op jit(solution)/shard_map/ppermute | solution.py:448
  235.2 33.5 %collective-permute-start.36 = (bf16[512,768]{1,0:T(8,128)(2,1)S(1)}, bf16[512,768]{1,0:T(8,128)(2,1)S(1)}, u32[]{:S(2)}, u32[]{:S(2)}) collective-permute-start(bf16[512,768]{1,0:T(8,128)(2,1)S(1)} %get-tuple-element.149), channel_id=1, source_target_pairs={{16,8},{8,0},{17,9},{9,1},{18,10},{10,2},{19,11},{11,3},{20,12},{1... | collective-permute-start | bytes 2359304 | tf_op jit(solution)/shard_map/ppermute | solution.py:453
  245.9 28.2 %collective-permute-start.37 = (bf16[512,768]{1,0:T(8,128)(2,1)S(1)}, bf16[512,768]{1,0:T(8,128)(2,1)S(1)}, u32[]{:S(2)}, u32[]{:S(2)}) collective-permute-start(bf16[512,768]{1,0:T(8,128)(2,1)S(1)} %get-tuple-element.156), channel_id=1, source_target_pairs={{8,16},{16,24},{9,17},{17,25},{10,18},{18,26},{11,19},{19,27},{12,... | collective-permute-start | bytes 2359304 | tf_op jit(solution)/shard_map/ppermute | solution.py:448
  252.0 33.5 %collective-permute-start.38 = (bf16[512,768]{1,0:T(8,128)(2,1)S(1)}, bf16[512,768]{1,0:T(8,128)(2,1)S(1)}, u32[]{:S(2)}, u32[]{:S(2)}) collective-permute-start(bf16[512,768]{1,0:T(8,128)(2,1)S(1)} %get-tuple-element.159), channel_id=1, source_target_pairs={{16,8},{8,0},{17,9},{9,1},{18,10},{10,2},{19,11},{11,3},{20,12},{1... | collective-permute-start | bytes 2359304 | tf_op jit(solution)/shard_map/ppermute | solution.py:453
  262.0 29.7 %collective-permute-start.39 = (bf16[512,768]{1,0:T(8,128)(2,1)S(1)}, bf16[512,768]{1,0:T(8,128)(2,1)S(1)}, u32[]{:S(2)}, u32[]{:S(2)}) collective-permute-start(bf16[512,768]{1,0:T(8,128)(2,1)S(1)} %get-tuple-element.166), channel_id=1, source_target_pairs={{16,24},{17,25},{18,26},{19,27},{20,28},{21,29},{22,30},{23,31}} | collective-permute-start | bytes 2359304 | tf_op jit(solution)/shard_map/ppermute | solution.py:448
  268.9 33.5 %collective-permute-start.40 = (bf16[512,768]{1,0:T(8,128)(2,1)S(1)}, bf16[512,768]{1,0:T(8,128)(2,1)S(1)}, u32[]{:S(2)}, u32[]{:S(2)}) collective-permute-start(bf16[512,768]{1,0:T(8,128)(2,1)S(1)} %get-tuple-element.169), channel_id=1, source_target_pairs={{8,0},{9,1},{10,2},{11,3},{12,4},{13,5},{14,6},{15,7}} | collective-permute-start | bytes 2359304 | tf_op jit(solution)/shard_map/ppermute | solution.py:453
  274.2 29.8 %collective-permute-start.43 = (bf16[512,768]{1,0:T(8,128)(2,1)S(1)}, bf16[512,768]{1,0:T(8,128)(2,1)S(1)}, u32[]{:S(2)}, u32[]{:S(2)}) collective-permute-start(bf16[512,768]{1,0:T(8,128)(2,1)S(1)} %get-tuple-element.172), channel_id=1, source_target_pairs={{16,24},{17,25},{18,26},{19,27},{20,28},{21,29},{22,30},{23,31}} | collective-permute-start | bytes 2359304 | tf_op jit(solution)/shard_map/ppermute | solution.py:448
  285.7 32.8 %collective-permute-start.44 = (bf16[512,768]{1,0:T(8,128)(2,1)S(1)}, bf16[512,768]{1,0:T(8,128)(2,1)S(1)}, u32[]{:S(2)}, u32[]{:S(2)}) collective-permute-start(bf16[512,768]{1,0:T(8,128)(2,1)S(1)} %get-tuple-element.175), channel_id=1, source_target_pairs={{8,0},{9,1},{10,2},{11,3},{12,4},{13,5},{14,6},{15,7}} | collective-permute-start | bytes 2359304 | tf_op jit(solution)/shard_map/ppermute | solution.py:453
  302.3 26.9 %collective-permute-start.47 = (bf16[8,128,256]{2,1,0:T(8,128)(2,1)S(1)}, bf16[8,128,256]{2,1,0:T(8,128)(2,1)S(1)}, u32[]{:S(2)}, u32[]{:S(2)}) collective-permute-start(bf16[8,128,256]{2,1,0:T(8,128)(2,1)S(1)} %get-tuple-element.180), channel_id=1, source_target_pairs={{0,16},{1,17},{2,18},{3,19},{4,20},{5,21},{6,22},{7,23}} | collective-permute-start | bytes 1572872 | tf_op jit(solution)/shard_map/ppermute | solution.py:473
  (72 other events, 1162.2 us)
where the time goes:
time: 368 us; the launch traced here: 366 us
  waiting for transfers between devices  145 us (39%)
  Pallas kernels  96.3 us (26%)
  starting transfers between devices  86.3 us (23%)
  local copies, waits for them, and re-layouts  16.6 us (5%)
  blocking collectives  11.4 us (3%)
  other arithmetic  8.54 us (2%)
    pallas_call x16, Pallas kernels, term(): pl.pallas_call(term_kernel, out_shape=jax.ShapeDtypeStruct((rows, width),...  45.7 us
    ppermute x12, waiting for transfers between devices, shards(): lax.ppermute(sent_down, 'z', [(Z - 1 - s, Z - 2 - s) for s in slots if s...  40.5 us
    ppermute x3, waiting for transfers between devices, moved(): lax.ppermute(p, 'x', ring('x', k + 1))  37.9 us
    ppermute x12, starting transfers between devices, shards(): lax.ppermute(sent_up, 'z', [(s, s + 1) for s in slots if s + 1 < Z])  37.2 us
    pallas_call x4, Pallas kernels, run_conv(): pl.pallas_call(conv_kernel, out_shape=(jax.ShapeDtypeStruct((blocks, rows...  25.1 us
    ppermute x12, waiting for transfers between devices, shards(): lax.ppermute(sent_up, 'z', [(s, s + 1) for s in slots if s + 1 < Z])  19.4 us
    ppermute x4, waiting for transfers between devices, gather_rel(): lax.ppermute(value, axis, ring(axis, k))  16.9 us
    ppermute x4, waiting for transfers between devices, second_step(): lax.ppermute(value, axis, ring(axis, j))  14.7 us
  transfers between devices with their start and end apart: 51, of which 18 were waited for; matrix products, arithmetic and copies ran while one was open for 2% of the time, Pallas kernels for 24%

commit v1 on v0

--- a/solution.py
+++ b/solution.py
@@ -105,7 +105,7 @@
                 pltpu.VMEM((width // lane, rows * 8, lane), jnp.float32),
             ],
         ),
-        compiler_params=pltpu.CompilerParams(vmem_limit_bytes=24 * 1024 * 1024),
+        compiler_params=pltpu.CompilerParams(vmem_limit_bytes=16 * 1024 * 1024),
         cost_estimate=pl.CostEstimate(flops=0, bytes_accessed=0, transcendentals=0),
         name="conv",
     )(order, pick, *(p.reshape(-1, rows, width3) for p in parts), taps, decay, scaled, state, halo)
@@ -209,7 +209,7 @@
         out_specs=[vmem] * len(outs),
         scratch_shapes=[pltpu.VMEM((rows, width3), jnp.float32), pltpu.SemaphoreType.DMA],
         input_output_aliases=aliases,
-        compiler_params=pltpu.CompilerParams(vmem_limit_bytes=16 * 1024 * 1024),
+        compiler_params=pltpu.CompilerParams(vmem_limit_bytes=8 * 1024 * 1024),
         cost_estimate=pl.CostEstimate(flops=0, bytes_accessed=0, transcendentals=0),
         name="chain",
     )(*inputs)
@@ -237,7 +237,7 @@
         in_specs=[pl.BlockSpec(b.shape, lambda n: (0, 0)) for b in blocks]
         + [pl.BlockSpec((depth, step), lambda n: (0, n))],
         out_specs=pl.BlockSpec((rows, step), lambda n: (0, n)),
-        compiler_params=pltpu.CompilerParams(vmem_limit_bytes=32 * 1024 * 1024),
+        compiler_params=pltpu.CompilerParams(vmem_limit_bytes=16 * 1024 * 1024),
         cost_estimate=pl.CostEstimate(flops=0, bytes_accessed=0, transcendentals=0),
         name="term",
     )(*blocks, weight)
@@ -324,28 +324,6 @@
     near_sends = [sends(near_block, 0, 1), sends(near_block, 1, 2)]
     near_got = [moved([after(p, *far_got) for p in near_sends[0]]), None]
     kept = [cut_weight(weight, 2 * x + block, half) for block in (far_block, near_block)]
-    split = list(after(split, *near_got[0], *near_sends[1], *kept))
-    far_weight = assemble(kept[0], far_got)
-    near_weight = None
-
-    pairs, others = [], []
-    sent_ups = []
-
-    def first_step(k, *before):
-        pairs.append(gather_rel(after(split[k], *before), "xy"[k % 2]))
-
-    def second_step(k, *before):
-        axis = "yx"[k % 2]
-        value = after(pairs[k], *before)
-        others.append([lax.ppermute(value, axis, ring(axis, j)) for j in range(1, lax.axis_size(axis))])
-
-    def add_planes(k):
-        planes = range(k, min(k + 2, Z))
-        for i in planes:
-            first_step(i, *sent_ups[max(0, k - 2) : k - 1])
-        for i in planes:
-            second_step(i, *(sent_ups[k - 1 + i % 2 : k + i % 2] if k else []))
-
     def places(*sizes):
         grids = jnp.meshgrid(*(jnp.arange(n, dtype=jnp.int32) for n in sizes), indexing="ij")
         return [g.reshape(-1) for g in grids]
@@ -353,6 +331,7 @@
     bx, by, bc = places(X, Y, C)
     rel_x, rel_y, rel_c = (x - bx) % X, (y - by) % Y, (c - bc) % C
     group_rows = X * Y * C * share
+    unit_rows = group_rows * Z // 8
     lead = [C * (X, Y)[k % 2] * share for k in range(Z)]
 
     def rows_of(k):
@@ -370,10 +349,40 @@
     decay = near_cut(jnp.exp(-decay_rates))
     scaled = near_cut(residues * jnp.sqrt(2.0 * decay_rates))
 
-    unit_rows = group_rows * Z // 8
-    count = group_rows * Z // unit_rows
     place_up = jnp.reshape(z, (1,)).astype(jnp.int32)
     place_down = Z - 1 - place_up
+    orders = []
+    for k in range(Z):
+        first = 0 if k < 2 else k * group_rows // unit_rows
+        rows = rows_of(k) - first * unit_rows
+        orders.append((first, rows % unit_rows // share, rows // unit_rows))
+    small = [taps, decay, scaled, place_up, place_down] + [v for o in orders for v in o[1:]]
+
+    far_weight = assemble(kept[0], far_got)
+    split = list(after(split, far_weight, *near_got[0], *near_sends[1], *kept, *small))
+    near_weight = None
+
+    pairs, others = [], []
+    sent_ups = []
+
+    def first_step(k, *before):
+        pairs.append(gather_rel(after(split[k], *before), "xy"[k % 2]))
+
+    def second_step(k, *before):
+        axis = "yx"[k % 2]
+        value = after(pairs[k], *before)
+        others.append([lax.ppermute(value, axis, ring(axis, j)) for j in range(1, lax.axis_size(axis))])
+
+    def add_planes(k):
+        planes = range(k, min(k + 2, Z))
+        for i in planes:
+            first_step(i, *sent_ups[max(0, k - 2) : k - 1])
+        if k == 0:
+            pairs[:] = lax.optimization_barrier(tuple(pairs))
+        for i in planes:
+            second_step(i, *(sent_ups[k - 1 + i % 2 : k + i % 2] if k else []))
+
+    count = group_rows * Z // unit_rows
     far, near = {}, {}
     ups, downs = {}, {}
     totals = []
@@ -419,12 +428,9 @@
 
     def emit(plane):
         nonlocal state, halo
-        first = 0 if plane < 2 else plane * group_rows
-        begin, end = first // unit_rows, -(-ready(plane) // unit_rows)
-        rows = rows_of(plane) - begin * unit_rows
-        out, state, halo = run_conv(
-            rows % unit_rows // share, rows // unit_rows, totals[begin:end], share, taps, decay, scaled, state, halo
-        )
+        first, order, pick = orders[plane]
+        parts = totals[first : -(-ready(plane) // unit_rows)]
+        out, state, halo = run_conv(order, pick, parts, share, taps, decay, scaled, state, halo)
         outs.append(out.reshape(X * Y * C, share, half))
         return out
 
@@ -477,7 +483,8 @@
     def spread(total):
         return lax.all_to_all(total, ("x", "y", "c"), split_axis=0, concat_axis=0, tiled=True)
 
-    return join(spread(collect(Z - 1)), spread(collect(0)), (X, Y, C))
+    upper = spread(collect(Z - 1))
+    return join(upper, spread(after(collect(0), upper)), (X, Y, C))
 
 
 def solution(mesh):

time: 368 us -> 361 us (0.981)
  waiting for transfers between devices: 145 us -> 161 us
  Pallas kernels: 96.3 us -> 82.4 us
  local copies, waits for them, and re-layouts: 16.6 us -> 4.03 us
    ppermute x12, waiting for transfers between devices: 40.5 us -> 52.1 us  [shards(): lax.ppermute(sent_down, 'z', [(Z - 1 - s, Z - 2 - s) for s in slots if s...]
    unnamed x94 -> x20, local copies, waits for them, and re-layouts: 13.4 us -> 1.93 us
    ppermute x12, waiting for transfers between devices: 19.4 us -> 28.3 us  [shards(): lax.ppermute(sent_up, 'z', [(s, s + 1) for s in slots if s + 1 < Z])]
    pallas_call x28, Pallas kernels: 13 us -> 5.25 us  [run_chain(): pl.pallas_call(functools.partial(chain_kernel, tuple(slots), planes, got...]
    ppermute x4, starting transfers between devices: 5.37 us -> 11.4 us  [collect(): came[home, k] = lax.ppermute(value, 'z', [(home, k)])]
    ppermute x4, waiting for transfers between devices: 10.4 us -> 4.65 us  [collect(): came[home, k] = lax.ppermute(value, 'z', [(home, k)])]
    pallas_call x16, Pallas kernels: 45.7 us -> 40.2 us  [term(): pl.pallas_call(term_kernel, out_shape=jax.ShapeDtypeStruct((rows, width),...]
  transfers between devices with their start and end apart: 51 -> 51, of which waited for: 18 -> 26; matrix products, arithmetic and copies ran while one was open for 2% -> 3% of each run, Pallas kernels for 24% -> 21%
where the time goes in v1:
time: 361 us; the launch traced here: 360 us
  waiting for transfers between devices  161 us (45%)
  starting transfers between devices  89.4 us (25%)
  Pallas kernels  82.4 us (23%)
  blocking collectives  11.4 us (3%)
  other arithmetic  10.4 us (3%)
  local copies, waits for them, and re-layouts  4.03 us (1%)
    ppermute x12, waiting for transfers between devices, shards(): lax.ppermute(sent_down, 'z', [(Z - 1 - s, Z - 2 - s) for s in slots if s...  52.1 us
    pallas_call x16, Pallas kernels, term(): pl.pallas_call(term_kernel, out_shape=jax.ShapeDtypeStruct((rows, width),...  40.2 us
    ppermute x12, starting transfers between devices, shards(): lax.ppermute(sent_up, 'z', [(s, s + 1) for s in slots if s + 1 < Z])  35.6 us
    ppermute x3, waiting for transfers between devices, moved(): lax.ppermute(p, 'x', ring('x', k + 1))  35.2 us
    ppermute x12, waiting for transfers between devices, shards(): lax.ppermute(sent_up, 'z', [(s, s + 1) for s in slots if s + 1 < Z])  28.3 us
    pallas_call x4, Pallas kernels, run_conv(): pl.pallas_call(conv_kernel, out_shape=(jax.ShapeDtypeStruct((blocks, rows...  24.5 us
    ppermute x4, waiting for transfers between devices, gather_rel(): lax.ppermute(value, axis, ring(axis, k))  19.5 us
    ppermute x4, waiting for transfers between devices, second_step(): lax.ppermute(value, axis, ring(axis, j))  17.4 us
  transfers between devices with their start and end apart: 51, of which 26 were waited for; matrix products, arithmetic and copies ran while one was open for 3% of the time, Pallas kernels for 21%

profile of v1, /device:TPU:0, one launch (start us, length us, event | category | flops | bytes accessed | tf_op | source)
XLA Modules:
  0.0 359.6 jit_solution(6925652465503629257)
XLA Ops:
  4.5 6.3 %all-to-all-start = ((bf16[4,128,2048]{2,1,0:T(8,128)(2,1)}), bf16[4,128,2048]{2,1,0:T(8,128)(2,1)}, u32[]{:S(2)}, u32[]{:S(2)}) async-start(bf16[4,128,2048]{2,1,0:T(8,128)(2,1)} %cut_tokens.1), calls=%async_computation | async-start | bytes 4194304 | tf_op jit(solution)/shard_map/all_to_all | solution.py:323
  20.8 26.0 %collective-permute-done = bf16[1024,768]{1,0:T(8,128)(2,1)} collective-permute-done((bf16[1024,768]{1,0:T(8,128)(2,1)S(1)}, bf16[1024,768]{1,0:T(8,128)(2,1)}, u32[]{:S(2)}, u32[]{:S(2)}) %collective-permute-start) | collective-permute-done | bytes 1572896 | tf_op jit(solution)/shard_map/ppermute | solution.py:307
  50.1 9.2 %collective-permute-done.1 = bf16[1024,256]{1,0:T(8,128)(2,1)} collective-permute-done((bf16[1024,256]{1,0:T(8,128)(2,1)S(1)}, bf16[1024,256]{1,0:T(8,128)(2,1)}, u32[]{:S(2)}, u32[]{:S(2)}) %collective-permute-start.1) | collective-permute-done | bytes 524320 | tf_op jit(solution)/shard_map/ppermute | solution.py:307
  64.2 9.6 %collective-permute-done.3 = bf16[128,2048]{1,0:T(8,128)(2,1)S(1)} collective-permute-done((bf16[128,2048]{1,0:T(8,128)(2,1)S(1)}, bf16[128,2048]{1,0:T(8,128)(2,1)S(1)}, u32[]{:S(2)}, u32[]{:S(2)}) %collective-permute-start.3) | collective-permute-done | bytes 524320 | tf_op jit(solution)/shard_map/ppermute | solution.py:284
  84.2 17.1 %collective-permute-done.10.refs_0_ = bf16[256,2048]{1,0:T(8,128)(2,1)S(1)} collective-permute-done((bf16[256,2048]{1,0:T(8,128)(2,1)S(1)}, bf16[256,2048]{1,0:T(8,128)(2,1)S(1)}, u32[]{:S(2)}, u32[]{:S(2)}) %collective-permute-start.10) | collective-permute-done | bytes 1048608 | tf_op jit(solution)/shard_map/ppermute | solution.py:374
  105.6 6.5 %collective-permute-done.14 = bf16[128,2048]{1,0:T(8,128)(2,1)S(1)} collective-permute-done((bf16[128,2048]{1,0:T(8,128)(2,1)S(1)}, bf16[128,2048]{1,0:T(8,128)(2,1)S(1)}, u32[]{:S(2)}, u32[]{:S(2)}) %collective-permute-start.14) | collective-permute-done | bytes 524320 | tf_op jit(solution)/shard_map/ppermute | solution.py:284
  124.8 8.4 %collective-permute-done.12.refs_2_ = bf16[512,768]{1,0:T(8,128)(2,1)S(1)} collective-permute-done((bf16[512,768]{1,0:T(8,128)(2,1)S(1)}, bf16[512,768]{1,0:T(8,128)(2,1)S(1)}, u32[]{:S(2)}, u32[]{:S(2)}) %collective-permute-start.12) | collective-permute-done | bytes 786464 | tf_op jit(solution)/shard_map/ppermute | solution.py:454
  156.7 5.0 %collective-permute-start.25 = (bf16[512,768]{1,0:T(8,128)(2,1)S(1)}, bf16[512,768]{1,0:T(8,128)(2,1)S(1)}, u32[]{:S(2)}, u32[]{:S(2)}) collective-permute-start(bf16[512,768]{1,0:T(8,128)(2,1)S(1)} %chain.36), channel_id=1, source_target_pairs={{0,8},{8,16},{16,24},{1,9},{9,17},{17,25},{2,10},{10,18},{18,26},{... | collective-permute-start | bytes 2359304 | tf_op jit(solution)/shard_map/ppermute | solution.py:454
  167.0 5.4 %collective-permute-done.21.refs_3_ = bf16[512,768]{1,0:T(8,128)(2,1)S(1)} collective-permute-done((bf16[512,768]{1,0:T(8,128)(2,1)S(1)}, bf16[512,768]{1,0:T(8,128)(2,1)S(1)}, u32[]{:S(2)}, u32[]{:S(2)}) %collective-permute-start.21) | collective-permute-done | bytes 786464 | tf_op jit(solution)/shard_map/ppermute | solution.py:454
  174.2 8.1 %collective-permute-start.29 = (bf16[512,768]{1,0:T(8,128)(2,1)S(1)}, bf16[512,768]{1,0:T(8,128)(2,1)S(1)}, u32[]{:S(2)}, u32[]{:S(2)}) collective-permute-start(bf16[512,768]{1,0:T(8,128)(2,1)S(1)} %chain.38), channel_id=1, source_target_pairs={{0,8},{8,16},{16,24},{1,9},{9,17},{17,25},{2,10},{10,18},{18,26},{... | collective-permute-start | bytes 2359304 | tf_op jit(solution)/shard_map/ppermute | solution.py:454
  189.6 4.4 %collective-permute-start.31 = (bf16[512,768]{1,0:T(8,128)(2,1)S(1)}, bf16[512,768]{1,0:T(8,128)(2,1)S(1)}, u32[]{:S(2)}, u32[]{:S(2)}) collective-permute-start(bf16[512,768]{1,0:T(8,128)(2,1)S(1)} %get-tuple-element.136), channel_id=1, source_target_pairs={{0,8},{8,16},{16,24},{1,9},{9,17},{17,25},{2,10},{10,18},{18,26},{... | collective-permute-start | bytes 2359304 | tf_op jit(solution)/shard_map/ppermute | solution.py:454
  216.6 6.4 %collective-permute-done.31.refs_3_ = bf16[512,768]{1,0:T(8,128)(2,1)S(1)} collective-permute-done((bf16[512,768]{1,0:T(8,128)(2,1)S(1)}, bf16[512,768]{1,0:T(8,128)(2,1)S(1)}, u32[]{:S(2)}, u32[]{:S(2)}) %collective-permute-start.31) | collective-permute-done | bytes 786464 | tf_op jit(solution)/shard_map/ppermute | solution.py:454
  223.7 5.6 %collective-permute-done.32.refs_3_ = bf16[512,768]{1,0:T(8,128)(2,1)S(1)} collective-permute-done((bf16[512,768]{1,0:T(8,128)(2,1)S(1)}, bf16[512,768]{1,0:T(8,128)(2,1)S(1)}, u32[]{:S(2)}, u32[]{:S(2)}) %collective-permute-start.32) | collective-permute-done | bytes 786464 | tf_op jit(solution)/shard_map/ppermute | solution.py:459
  231.0 6.0 %conv.4 = (bf16[8,128,256]{2,1,0:T(8,128)(2,1)S(1)}, f32[16,256]{1,0:T(8,128)S(1)}, f32[8,768]{1,0:T(8,128)S(1)}) custom-call(s32[8]{0:T(128)S(1)} %get-tuple-element.222.order, s32[8]{0:T(128)S(1)} %get-tuple-element.218.pick, f32[4,128,768]{2,1,0:T(8,128)S(1)} %bitcast.30, f32[4,128,768]{2,1,0:T(8,128)S(1)} %bitcast.32, f32[4,128,768]{2,1,0:T(8,128)S(1)} %bitcast.26, ...), custom_call_target="tpu_custom_call" | custom-call | tf_op jit(solution)/shard_map/conv/pallas_call | solution.py:79
  240.3 5.9 %collective-permute-done.34.refs_3_ = bf16[512,768]{1,0:T(8,128)(2,1)S(1)} collective-permute-done((bf16[512,768]{1,0:T(8,128)(2,1)S(1)}, bf16[512,768]{1,0:T(8,128)(2,1)S(1)}, u32[]{:S(2)}, u32[]{:S(2)}) %collective-permute-start.34) | collective-permute-done | bytes 786464 | tf_op jit(solution)/shard_map/ppermute | solution.py:459
  247.8 6.1 %conv.5 = (bf16[8,128,256]{2,1,0:T(8,128)(2,1)S(1)}, f32[16,256]{1,0:T(8,128)S(1)}, f32[8,768]{1,0:T(8,128)S(1)}) custom-call(s32[8]{0:T(128)S(1)} %get-tuple-element.221.order, s32[8]{0:T(128)S(1)} %get-tuple-element.200.pick, f32[4,128,768]{2,1,0:T(8,128)S(1)} %bitcast.31, f32[4,128,768]{2,1,0:T(8,128)S(1)} %bitcast.33, f32[4,128,768]{2,1,0:T(8,128)S(1)} %bitcast.27, ...), custom_call_target="tpu_custom_call" | custom-call | tf_op jit(solution)/shard_map/conv/pallas_call | solution.py:79
  257.2 5.9 %collective-permute-done.36.refs_2_ = bf16[512,768]{1,0:T(8,128)(2,1)S(1)} collective-permute-done((bf16[512,768]{1,0:T(8,128)(2,1)S(1)}, bf16[512,768]{1,0:T(8,128)(2,1)S(1)}, u32[]{:S(2)}, u32[]{:S(2)}) %collective-permute-start.36) | collective-permute-done | bytes 786464 | tf_op jit(solution)/shard_map/ppermute | solution.py:459
  267.9 12.0 %collective-permute-done.38.refs_2_ = bf16[512,768]{1,0:T(8,128)(2,1)S(1)} collective-permute-done((bf16[512,768]{1,0:T(8,128)(2,1)S(1)}, bf16[512,768]{1,0:T(8,128)(2,1)S(1)}, u32[]{:S(2)}, u32[]{:S(2)}) %collective-permute-start.38) | collective-permute-done | bytes 786464 | tf_op jit(solution)/shard_map/ppermute | solution.py:459
  281.5 4.6 %collective-permute-start.41 = (bf16[8,128,256]{2,1,0:T(8,128)(2,1)S(1)}, bf16[8,128,256]{2,1,0:T(8,128)(2,1)S(1)}, u32[]{:S(2)}, u32[]{:S(2)}) collective-permute-start(bf16[8,128,256]{2,1,0:T(8,128)(2,1)S(1)} %get-tuple-element.168), channel_id=1, source_target_pairs={{0,8},{1,9},{2,10},{3,11},{4,12},{5,13},{6,14},{7,15}} | collective-permute-start | bytes 1572872 | tf_op jit(solution)/shard_map/ppermute | solution.py:468
  286.8 5.9 %conv.6 = (bf16[8,128,256]{2,1,0:T(8,128)(2,1)S(1)}, f32[16,256]{1,0:T(8,128)S(1)}, f32[8,768]{1,0:T(8,128)S(1)}) custom-call(s32[8]{0:T(128)S(1)} %get-tuple-element.220.order, s32[8]{0:T(128)S(1)} %get-tuple-element.216.pick, f32[4,128,768]{2,1,0:T(8,128)S(1)} %bitcast.35, f32[4,128,768]{2,1,0:T(8,128)S(1)} %bitcast.36, f32[3,768]{1,0:T(4,128)S(1)} %bitcast.39, ...), custom_call_target="tpu_custom_call" | custom-call | tf_op jit(solution)/shard_map/conv/pallas_call | solution.py:79
  297.8 15.6 %collective-permute-done.44.refs_1_ = bf16[512,768]{1,0:T(8,128)(2,1)S(1)} collective-permute-done((bf16[512,768]{1,0:T(8,128)(2,1)S(1)}, bf16[512,768]{1,0:T(8,128)(2,1)S(1)}, u32[]{:S(2)}, u32[]{:S(2)}) %collective-permute-start.44) | collective-permute-done | bytes 786464 | tf_op jit(solution)/shard_map/ppermute | solution.py:459
  317.1 6.4 %conv.7 = (bf16[8,128,256]{2,1,0:T(8,128)(2,1)S(1)}, f32[16,256]{1,0:T(8,128)}, f32[8,768]{1,0:T(8,128)}) custom-call(s32[8]{0:T(128)S(1)} %get-tuple-element.223.order, s32[8]{0:T(128)S(1)} %get-tuple-element.195.pick, f32[4,128,768]{2,1,0:T(8,128)S(1)} %bitcast.28, f32[4,128,768]{2,1,0:T(8,128)S(1)} %bitcast.29, f32[3,768]{1,0:T(4,128)S(1)} %bitcast.40, ...), custom_call_target="tpu_custom_call" | custom-call | tf_op jit(solution)/shard_map/conv/pallas_call | solution.py:79
  323.5 7.3 %collective-permute-start.48 = (bf16[8,128,256]{2,1,0:T(8,128)(2,1)S(1)}, bf16[8,128,256]{2,1,0:T(8,128)(2,1)}, u32[]{:S(2)}, u32[]{:S(2)}) collective-permute-start(bf16[8,128,256]{2,1,0:T(8,128)(2,1)S(1)} %get-tuple-element.192), channel_id=1, source_target_pairs={{0,24},{1,25},{2,26},{3,27},{4,28},{5,29},{6,30},{7,31}} | collective-permute-start | bytes 1572872 | tf_op jit(solution)/shard_map/ppermute | solution.py:479
  345.5 11.4 %all_to_all.15.second = bf16[8,128,256]{2,1,0:T(8,128)(2,1)S(1)} all-to-all(bf16[8,128,256]{2,1,0:T(8,128)(2,1)S(1)} %add_add_fusion), channel_id=1, replica_groups=mesh['z'=4,'x'=2,'y'=2,'c'=2] {'x','y','c'}, dimensions={0} | all-to-all | bytes 1048576 | tf_op jit(solution)/shard_map/all_to_all | solution.py:484
  (179 shorter events, 153.3 us)
Async XLA Ops:
  4.5 54.9 %all-to-all-start = ((bf16[4,128,2048]{2,1,0:T(8,128)(2,1)}), bf16[4,128,2048]{2,1,0:T(8,128)(2,1)}, u32[]{:S(2)}, u32[]{:S(2)}) async-start(bf16[4,128,2048]{2,1,0:T(8,128)(2,1)} %cut_tokens.1), calls=%async_computation | async-start | bytes 4194304 | tf_op jit(solution)/shard_map/all_to_all | solution.py:323
  10.8 36.0 %collective-permute-start = (bf16[1024,768]{1,0:T(8,128)(2,1)S(1)}, bf16[1024,768]{1,0:T(8,128)(2,1)}, u32[]{:S(2)}, u32[]{:S(2)}) collective-permute-start(bf16[1024,768]{1,0:T(8,128)(2,1)S(1)} %cut_weight.5), channel_id=1, source_target_pairs={{0,4},{4,0},{1,5},{5,1},{2,6},{6,2},{3,7},{7,3},{8,12},{12,8},{9,1... | collective-permute-start | bytes 4718600 | tf_op jit(solution)/shard_map/ppermute | solution.py:307
  80.8 31.2 %collective-permute-start.14 = (bf16[128,2048]{1,0:T(8,128)(2,1)S(1)}, bf16[128,2048]{1,0:T(8,128)(2,1)S(1)}, u32[]{:S(2)}, u32[]{:S(2)}) collective-permute-start(bf16[128,2048]{1,0:T(8,128)(2,1)S(1)} %get-tuple-element.118), channel_id=1, source_target_pairs={{0,4},{4,0},{1,5},{5,1},{2,6},{6,2},{3,7},{7,3},{8,12},{12,8},{9,1... | collective-permute-start | bytes 1572872 | tf_op jit(solution)/shard_map/ppermute | solution.py:284
  82.3 33.5 %collective-permute-start.8 = (bf16[512,768]{1,0:T(8,128)(2,1)S(1)}, bf16[512,768]{1,0:T(8,128)(2,1)S(1)}, u32[]{:S(2)}, u32[]{:S(2)}) collective-permute-start(bf16[512,768]{1,0:T(8,128)(2,1)S(1)} %chain.28), channel_id=1, source_target_pairs={{0,8},{1,9},{2,10},{3,11},{4,12},{5,13},{6,14},{7,15}} | collective-permute-start | bytes 2359304 | tf_op jit(solution)/shard_map/ppermute | solution.py:454
  141.5 31.3 %collective-permute-start.27 = (bf16[256,2048]{1,0:T(8,128)(2,1)S(1)}, bf16[256,2048]{1,0:T(8,128)(2,1)S(1)}, u32[]{:S(2)}, u32[]{:S(2)}) collective-permute-start(bf16[256,2048]{1,0:T(8,128)(2,1)S(1)} %constant_dynamic-update-slice_fusion.2.refs_0_), channel_id=1, source_target_pairs={{0,4},{4,0},{1,5},{5,1},{2,6},{6,2},{3,7},{7,3},{8,12},{12,8},{9,1... | collective-permute-start | bytes 3145736 | tf_op jit(solution)/shard_map/ppermute | solution.py:374
  144.2 28.2 %collective-permute-start.21 = (bf16[512,768]{1,0:T(8,128)(2,1)S(1)}, bf16[512,768]{1,0:T(8,128)(2,1)S(1)}, u32[]{:S(2)}, u32[]{:S(2)}) collective-permute-start(bf16[512,768]{1,0:T(8,128)(2,1)S(1)} %chain.34), channel_id=1, source_target_pairs={{0,8},{8,16},{1,9},{9,17},{2,10},{10,18},{3,11},{11,19},{4,12},{12... | collective-permute-start | bytes 2359304 | tf_op jit(solution)/shard_map/ppermute | solution.py:454
  155.9 26.4 %collective-permute-start.24 = (bf16[256,2048]{1,0:T(8,128)(2,1)S(1)}, bf16[256,2048]{1,0:T(8,128)(2,1)S(1)}, u32[]{:S(2)}, u32[]{:S(2)}) collective-permute-start(bf16[256,2048]{1,0:T(8,128)(2,1)S(1)} %constant_dynamic-update-slice_fusion.2.refs_0_), channel_id=1, source_target_pairs={{0,1},{1,0},{2,3},{3,2},{4,5},{5,4},{6,7},{7,6},{8,9},{9,8},{10,11... | collective-permute-start | bytes 3145736 | tf_op jit(solution)/shard_map/ppermute | solution.py:416
  156.7 32.5 %collective-permute-start.25 = (bf16[512,768]{1,0:T(8,128)(2,1)S(1)}, bf16[512,768]{1,0:T(8,128)(2,1)S(1)}, u32[]{:S(2)}, u32[]{:S(2)}) collective-permute-start(bf16[512,768]{1,0:T(8,128)(2,1)S(1)} %chain.36), channel_id=1, source_target_pairs={{0,8},{8,16},{16,24},{1,9},{9,17},{17,25},{2,10},{10,18},{18,26},{... | collective-permute-start | bytes 2359304 | tf_op jit(solution)/shard_map/ppermute | solution.py:454
  172.8 27.0 %collective-permute-start.28 = (bf16[256,2048]{1,0:T(8,128)(2,1)S(1)}, bf16[256,2048]{1,0:T(8,128)(2,1)S(1)}, u32[]{:S(2)}, u32[]{:S(2)}) collective-permute-start(bf16[256,2048]{1,0:T(8,128)(2,1)S(1)} %collective-permute-done.27.refs_0_), channel_id=1, source_target_pairs={{0,1},{1,0},{2,3},{3,2},{4,5},{5,4},{6,7},{7,6},{8,9},{9,8},{10,11... | collective-permute-start | bytes 3145736 | tf_op jit(solution)/shard_map/ppermute | solution.py:416
  174.2 32.0 %collective-permute-start.29 = (bf16[512,768]{1,0:T(8,128)(2,1)S(1)}, bf16[512,768]{1,0:T(8,128)(2,1)S(1)}, u32[]{:S(2)}, u32[]{:S(2)}) collective-permute-start(bf16[512,768]{1,0:T(8,128)(2,1)S(1)} %chain.38), channel_id=1, source_target_pairs={{0,8},{8,16},{16,24},{1,9},{9,17},{17,25},{2,10},{10,18},{18,26},{... | collective-permute-start | bytes 2359304 | tf_op jit(solution)/shard_map/ppermute | solution.py:454
  182.3 30.2 %collective-permute-start.30 = (bf16[512,768]{1,0:T(8,128)(2,1)S(1)}, bf16[512,768]{1,0:T(8,128)(2,1)S(1)}, u32[]{:S(2)}, u32[]{:S(2)}) collective-permute-start(bf16[512,768]{1,0:T(8,128)(2,1)S(1)} %chain.39), channel_id=1, source_target_pairs={{24,16},{16,8},{8,0},{25,17},{17,9},{9,1},{26,18},{18,10},{10,2},{... | collective-permute-start | bytes 2359304 | tf_op jit(solution)/shard_map/ppermute | solution.py:459
  189.6 33.3 %collective-permute-start.31 = (bf16[512,768]{1,0:T(8,128)(2,1)S(1)}, bf16[512,768]{1,0:T(8,128)(2,1)S(1)}, u32[]{:S(2)}, u32[]{:S(2)}) collective-permute-start(bf16[512,768]{1,0:T(8,128)(2,1)S(1)} %get-tuple-element.136), channel_id=1, source_target_pairs={{0,8},{8,16},{16,24},{1,9},{9,17},{17,25},{2,10},{10,18},{18,26},{... | collective-permute-start | bytes 2359304 | tf_op jit(solution)/shard_map/ppermute | solution.py:454
  195.9 33.4 %collective-permute-start.32 = (bf16[512,768]{1,0:T(8,128)(2,1)S(1)}, bf16[512,768]{1,0:T(8,128)(2,1)S(1)}, u32[]{:S(2)}, u32[]{:S(2)}) collective-permute-start(bf16[512,768]{1,0:T(8,128)(2,1)S(1)} %get-tuple-element.139), channel_id=1, source_target_pairs={{24,16},{16,8},{8,0},{25,17},{17,9},{9,1},{26,18},{18,10},{10,2},{... | collective-permute-start | bytes 2359304 | tf_op jit(solution)/shard_map/ppermute | solution.py:459
  206.4 33.1 %collective-permute-start.33 = (bf16[512,768]{1,0:T(8,128)(2,1)S(1)}, bf16[512,768]{1,0:T(8,128)(2,1)S(1)}, u32[]{:S(2)}, u32[]{:S(2)}) collective-permute-start(bf16[512,768]{1,0:T(8,128)(2,1)S(1)} %get-tuple-element.145), channel_id=1, source_target_pairs={{0,8},{8,16},{16,24},{1,9},{9,17},{17,25},{2,10},{10,18},{18,26},{... | collective-permute-start | bytes 2359304 | tf_op jit(solution)/shard_map/ppermute | solution.py:454
  212.8 33.4 %collective-permute-start.34 = (bf16[512,768]{1,0:T(8,128)(2,1)S(1)}, bf16[512,768]{1,0:T(8,128)(2,1)S(1)}, u32[]{:S(2)}, u32[]{:S(2)}) collective-permute-start(bf16[512,768]{1,0:T(8,128)(2,1)S(1)} %get-tuple-element.148), channel_id=1, source_target_pairs={{24,16},{16,8},{8,0},{25,17},{17,9},{9,1},{26,18},{18,10},{10,2},{... | collective-permute-start | bytes 2359304 | tf_op jit(solution)/shard_map/ppermute | solution.py:459
  223.0 33.4 %collective-permute-start.35 = (bf16[512,768]{1,0:T(8,128)(2,1)S(1)}, bf16[512,768]{1,0:T(8,128)(2,1)S(1)}, u32[]{:S(2)}, u32[]{:S(2)}) collective-permute-start(bf16[512,768]{1,0:T(8,128)(2,1)S(1)} %get-tuple-element.151), channel_id=1, source_target_pairs={{8,16},{16,24},{9,17},{17,25},{10,18},{18,26},{11,19},{19,27},{12,... | collective-permute-start | bytes 2359304 | tf_op jit(solution)/shard_map/ppermute | solution.py:454
  229.6 33.4 %collective-permute-start.36 = (bf16[512,768]{1,0:T(8,128)(2,1)S(1)}, bf16[512,768]{1,0:T(8,128)(2,1)S(1)}, u32[]{:S(2)}, u32[]{:S(2)}) collective-permute-start(bf16[512,768]{1,0:T(8,128)(2,1)S(1)} %get-tuple-element.154), channel_id=1, source_target_pairs={{16,8},{8,0},{17,9},{9,1},{18,10},{10,2},{19,11},{11,3},{20,12},{1... | collective-permute-start | bytes 2359304 | tf_op jit(solution)/shard_map/ppermute | solution.py:459
  239.5 27.6 %collective-permute-start.37 = (bf16[512,768]{1,0:T(8,128)(2,1)S(1)}, bf16[512,768]{1,0:T(8,128)(2,1)S(1)}, u32[]{:S(2)}, u32[]{:S(2)}) collective-permute-start(bf16[512,768]{1,0:T(8,128)(2,1)S(1)} %get-tuple-element.161), channel_id=1, source_target_pairs={{8,16},{16,24},{9,17},{17,25},{10,18},{18,26},{11,19},{19,27},{12,... | collective-permute-start | bytes 2359304 | tf_op jit(solution)/shard_map/ppermute | solution.py:454
  246.5 33.4 %collective-permute-start.38 = (bf16[512,768]{1,0:T(8,128)(2,1)S(1)}, bf16[512,768]{1,0:T(8,128)(2,1)S(1)}, u32[]{:S(2)}, u32[]{:S(2)}) collective-permute-start(bf16[512,768]{1,0:T(8,128)(2,1)S(1)} %get-tuple-element.164), channel_id=1, source_target_pairs={{16,8},{8,0},{17,9},{9,1},{18,10},{10,2},{19,11},{11,3},{20,12},{1... | collective-permute-start | bytes 2359304 | tf_op jit(solution)/shard_map/ppermute | solution.py:459
  256.5 29.7 %collective-permute-start.39 = (bf16[512,768]{1,0:T(8,128)(2,1)S(1)}, bf16[512,768]{1,0:T(8,128)(2,1)S(1)}, u32[]{:S(2)}, u32[]{:S(2)}) collective-permute-start(bf16[512,768]{1,0:T(8,128)(2,1)S(1)} %get-tuple-element.171), channel_id=1, source_target_pairs={{16,24},{17,25},{18,26},{19,27},{20,28},{21,29},{22,30},{23,31}} | collective-permute-start | bytes 2359304 | tf_op jit(solution)/shard_map/ppermute | solution.py:454
  263.3 33.4 %collective-permute-start.40 = (bf16[512,768]{1,0:T(8,128)(2,1)S(1)}, bf16[512,768]{1,0:T(8,128)(2,1)S(1)}, u32[]{:S(2)}, u32[]{:S(2)}) collective-permute-start(bf16[512,768]{1,0:T(8,128)(2,1)S(1)} %get-tuple-element.174), channel_id=1, source_target_pairs={{8,0},{9,1},{10,2},{11,3},{12,4},{13,5},{14,6},{15,7}} | collective-permute-start | bytes 2359304 | tf_op jit(solution)/shard_map/ppermute | solution.py:459
  267.2 30.6 %collective-permute-start.43 = (bf16[512,768]{1,0:T(8,128)(2,1)S(1)}, bf16[512,768]{1,0:T(8,128)(2,1)S(1)}, u32[]{:S(2)}, u32[]{:S(2)}) collective-permute-start(bf16[512,768]{1,0:T(8,128)(2,1)S(1)} %get-tuple-element.177), channel_id=1, source_target_pairs={{16,24},{17,25},{18,26},{19,27},{20,28},{21,29},{22,30},{23,31}} | collective-permute-start | bytes 2359304 | tf_op jit(solution)/shard_map/ppermute | solution.py:454
  280.2 33.2 %collective-permute-start.44 = (bf16[512,768]{1,0:T(8,128)(2,1)S(1)}, bf16[512,768]{1,0:T(8,128)(2,1)S(1)}, u32[]{:S(2)}, u32[]{:S(2)}) collective-permute-start(bf16[512,768]{1,0:T(8,128)(2,1)S(1)} %get-tuple-element.180), channel_id=1, source_target_pairs={{8,0},{9,1},{10,2},{11,3},{12,4},{13,5},{14,6},{15,7}} | collective-permute-start | bytes 2359304 | tf_op jit(solution)/shard_map/ppermute | solution.py:459
  296.7 34.1 %collective-permute-start.46 = (bf16[8,128,256]{2,1,0:T(8,128)(2,1)S(1)}, bf16[8,128,256]{2,1,0:T(8,128)(2,1)S(1)}, u32[]{:S(2)}, u32[]{:S(2)}) collective-permute-start(bf16[8,128,256]{2,1,0:T(8,128)(2,1)S(1)} %get-tuple-element.185), channel_id=1, source_target_pairs={{24,16},{25,17},{26,18},{27,19},{28,20},{29,21},{30,22},{31,23}} | collective-permute-start | bytes 1572872 | tf_op jit(solution)/shard_map/ppermute | solution.py:479
  (35 other events, 579.7 us)

commit v2 on v1

--- a/solution.py
+++ b/solution.py
@@ -317,9 +317,9 @@
         return jnp.concatenate(rows, axis=0)
 
     share = tok_rows // (Y * C)
+    mine = cut_tokens(tokens, y * C + c, Z, share)
     far_sends = sends(far_block)
-    far_got = moved(far_sends)
-    mine = cut_tokens(after(tokens, *far_sends), y * C + c, Z, share)
+    far_got = moved([after(p, mine) for p in far_sends])
     split = lax.all_to_all(mine, "z", split_axis=0, concat_axis=0, tiled=True)
     near_sends = [sends(near_block, 0, 1), sends(near_block, 1, 2)]
     near_got = [moved([after(p, *far_got) for p in near_sends[0]]), None]

time: 361 us -> 361 us (level)
  no operation moved by 1% of the time
where the time goes in v2:
time: 361 us; the launch traced here: 360 us
  waiting for transfers between devices  159 us (44%)
  starting transfers between devices  91.7 us (25%)
  Pallas kernels  82.4 us (23%)
  blocking collectives  11.4 us (3%)
  other arithmetic  10.4 us (3%)
  local copies, waits for them, and re-layouts  4.03 us (1%)
    ppermute x12, waiting for transfers between devices, shards(): lax.ppermute(sent_down, 'z', [(Z - 1 - s, Z - 2 - s) for s in slots if s...  52.1 us
    pallas_call x16, Pallas kernels, term(): pl.pallas_call(term_kernel, out_shape=jax.ShapeDtypeStruct((rows, width),...  40.1 us
    ppermute x12, starting transfers between devices, shards(): lax.ppermute(sent_up, 'z', [(s, s + 1) for s in slots if s + 1 < Z])  38.4 us
    ppermute x3, waiting for transfers between devices, moved(): lax.ppermute(p, 'x', ring('x', k + 1))  35.2 us
    ppermute x12, waiting for transfers between devices, shards(): lax.ppermute(sent_up, 'z', [(s, s + 1) for s in slots if s + 1 < Z])  28.3 us
    pallas_call x4, Pallas kernels, run_conv(): pl.pallas_call(conv_kernel, out_shape=(jax.ShapeDtypeStruct((blocks, rows...  24.5 us
    ppermute x4, waiting for transfers between devices, gather_rel(): lax.ppermute(value, axis, ring(axis, k))  18.4 us
    ppermute x4, waiting for transfers between devices, second_step(): lax.ppermute(value, axis, ring(axis, j))  16.3 us
  transfers between devices with their start and end apart: 51, of which 26 were waited for; matrix products, arithmetic and copies ran while one was open for 3% of the time, Pallas kernels for 21%

profile of v2, /device:TPU:0, one launch (start us, length us, event | category | flops | bytes accessed | tf_op | source)
XLA Modules:
  0.0 359.7 jit_solution(13137158262690347784)
XLA Ops:
  3.0 6.3 %all-to-all-start = ((bf16[4,128,2048]{2,1,0:T(8,128)(2,1)}), bf16[4,128,2048]{2,1,0:T(8,128)(2,1)}, u32[]{:S(2)}, u32[]{:S(2)}) async-start(bf16[4,128,2048]{2,1,0:T(8,128)(2,1)} %cut_tokens.1), calls=%async_computation | async-start | bytes 4194304 | tf_op jit(solution)/shard_map/all_to_all | solution.py:323
  20.9 26.0 %collective-permute-done = bf16[1024,768]{1,0:T(8,128)(2,1)} collective-permute-done((bf16[1024,768]{1,0:T(8,128)(2,1)S(1)}, bf16[1024,768]{1,0:T(8,128)(2,1)}, u32[]{:S(2)}, u32[]{:S(2)}) %collective-permute-start) | collective-permute-done | bytes 1572896 | tf_op jit(solution)/shard_map/ppermute | solution.py:307
  50.2 9.2 %collective-permute-done.1 = bf16[1024,256]{1,0:T(8,128)(2,1)} collective-permute-done((bf16[1024,256]{1,0:T(8,128)(2,1)S(1)}, bf16[1024,256]{1,0:T(8,128)(2,1)}, u32[]{:S(2)}, u32[]{:S(2)}) %collective-permute-start.1) | collective-permute-done | bytes 524320 | tf_op jit(solution)/shard_map/ppermute | solution.py:307
  64.3 8.5 %collective-permute-done.3 = bf16[128,2048]{1,0:T(8,128)(2,1)S(1)} collective-permute-done((bf16[128,2048]{1,0:T(8,128)(2,1)S(1)}, bf16[128,2048]{1,0:T(8,128)(2,1)S(1)}, u32[]{:S(2)}, u32[]{:S(2)}) %collective-permute-start.3) | collective-permute-done | bytes 524320 | tf_op jit(solution)/shard_map/ppermute | solution.py:284
  84.2 16.0 %collective-permute-done.10.refs_0_ = bf16[256,2048]{1,0:T(8,128)(2,1)S(1)} collective-permute-done((bf16[256,2048]{1,0:T(8,128)(2,1)S(1)}, bf16[256,2048]{1,0:T(8,128)(2,1)S(1)}, u32[]{:S(2)}, u32[]{:S(2)}) %collective-permute-start.10) | collective-permute-done | bytes 1048608 | tf_op jit(solution)/shard_map/ppermute | solution.py:374
  104.6 6.5 %collective-permute-done.14 = bf16[128,2048]{1,0:T(8,128)(2,1)S(1)} collective-permute-done((bf16[128,2048]{1,0:T(8,128)(2,1)S(1)}, bf16[128,2048]{1,0:T(8,128)(2,1)S(1)}, u32[]{:S(2)}, u32[]{:S(2)}) %collective-permute-start.14) | collective-permute-done | bytes 524320 | tf_op jit(solution)/shard_map/ppermute | solution.py:284
  124.9 8.4 %collective-permute-done.12.refs_2_ = bf16[512,768]{1,0:T(8,128)(2,1)S(1)} collective-permute-done((bf16[512,768]{1,0:T(8,128)(2,1)S(1)}, bf16[512,768]{1,0:T(8,128)(2,1)S(1)}, u32[]{:S(2)}, u32[]{:S(2)}) %collective-permute-start.12) | collective-permute-done | bytes 786464 | tf_op jit(solution)/shard_map/ppermute | solution.py:454
  156.8 5.0 %collective-permute-start.25 = (bf16[512,768]{1,0:T(8,128)(2,1)S(1)}, bf16[512,768]{1,0:T(8,128)(2,1)S(1)}, u32[]{:S(2)}, u32[]{:S(2)}) collective-permute-start(bf16[512,768]{1,0:T(8,128)(2,1)S(1)} %chain.36), channel_id=1, source_target_pairs={{0,8},{8,16},{16,24},{1,9},{9,17},{17,25},{2,10},{10,18},{18,26},{... | collective-permute-start | bytes 2359304 | tf_op jit(solution)/shard_map/ppermute | solution.py:454
  167.1 5.4 %collective-permute-done.21.refs_3_ = bf16[512,768]{1,0:T(8,128)(2,1)S(1)} collective-permute-done((bf16[512,768]{1,0:T(8,128)(2,1)S(1)}, bf16[512,768]{1,0:T(8,128)(2,1)S(1)}, u32[]{:S(2)}, u32[]{:S(2)}) %collective-permute-start.21) | collective-permute-done | bytes 786464 | tf_op jit(solution)/shard_map/ppermute | solution.py:454
  174.2 8.1 %collective-permute-start.29 = (bf16[512,768]{1,0:T(8,128)(2,1)S(1)}, bf16[512,768]{1,0:T(8,128)(2,1)S(1)}, u32[]{:S(2)}, u32[]{:S(2)}) collective-permute-start(bf16[512,768]{1,0:T(8,128)(2,1)S(1)} %chain.38), channel_id=1, source_target_pairs={{0,8},{8,16},{16,24},{1,9},{9,17},{17,25},{2,10},{10,18},{18,26},{... | collective-permute-start | bytes 2359304 | tf_op jit(solution)/shard_map/ppermute | solution.py:454
  189.7 4.4 %collective-permute-start.31 = (bf16[512,768]{1,0:T(8,128)(2,1)S(1)}, bf16[512,768]{1,0:T(8,128)(2,1)S(1)}, u32[]{:S(2)}, u32[]{:S(2)}) collective-permute-start(bf16[512,768]{1,0:T(8,128)(2,1)S(1)} %get-tuple-element.136), channel_id=1, source_target_pairs={{0,8},{8,16},{16,24},{1,9},{9,17},{17,25},{2,10},{10,18},{18,26},{... | collective-permute-start | bytes 2359304 | tf_op jit(solution)/shard_map/ppermute | solution.py:454
  216.7 6.4 %collective-permute-done.31.refs_3_ = bf16[512,768]{1,0:T(8,128)(2,1)S(1)} collective-permute-done((bf16[512,768]{1,0:T(8,128)(2,1)S(1)}, bf16[512,768]{1,0:T(8,128)(2,1)S(1)}, u32[]{:S(2)}, u32[]{:S(2)}) %collective-permute-start.31) | collective-permute-done | bytes 786464 | tf_op jit(solution)/shard_map/ppermute | solution.py:454
  223.8 5.6 %collective-permute-done.32.refs_3_ = bf16[512,768]{1,0:T(8,128)(2,1)S(1)} collective-permute-done((bf16[512,768]{1,0:T(8,128)(2,1)S(1)}, bf16[512,768]{1,0:T(8,128)(2,1)S(1)}, u32[]{:S(2)}, u32[]{:S(2)}) %collective-permute-start.32) | collective-permute-done | bytes 786464 | tf_op jit(solution)/shard_map/ppermute | solution.py:459
  231.0 6.0 %conv.4 = (bf16[8,128,256]{2,1,0:T(8,128)(2,1)S(1)}, f32[16,256]{1,0:T(8,128)S(1)}, f32[8,768]{1,0:T(8,128)S(1)}) custom-call(s32[8]{0:T(128)S(1)} %get-tuple-element.222.order, s32[8]{0:T(128)S(1)} %get-tuple-element.218.pick, f32[4,128,768]{2,1,0:T(8,128)S(1)} %bitcast.30, f32[4,128,768]{2,1,0:T(8,128)S(1)} %bitcast.32, f32[4,128,768]{2,1,0:T(8,128)S(1)} %bitcast.26, ...), custom_call_target="tpu_custom_call" | custom-call | tf_op jit(solution)/shard_map/conv/pallas_call | solution.py:79
  240.3 5.9 %collective-permute-done.34.refs_3_ = bf16[512,768]{1,0:T(8,128)(2,1)S(1)} collective-permute-done((bf16[512,768]{1,0:T(8,128)(2,1)S(1)}, bf16[512,768]{1,0:T(8,128)(2,1)S(1)}, u32[]{:S(2)}, u32[]{:S(2)}) %collective-permute-start.34) | collective-permute-done | bytes 786464 | tf_op jit(solution)/shard_map/ppermute | solution.py:459
  247.8 6.1 %conv.5 = (bf16[8,128,256]{2,1,0:T(8,128)(2,1)S(1)}, f32[16,256]{1,0:T(8,128)S(1)}, f32[8,768]{1,0:T(8,128)S(1)}) custom-call(s32[8]{0:T(128)S(1)} %get-tuple-element.221.order, s32[8]{0:T(128)S(1)} %get-tuple-element.200.pick, f32[4,128,768]{2,1,0:T(8,128)S(1)} %bitcast.31, f32[4,128,768]{2,1,0:T(8,128)S(1)} %bitcast.33, f32[4,128,768]{2,1,0:T(8,128)S(1)} %bitcast.27, ...), custom_call_target="tpu_custom_call" | custom-call | tf_op jit(solution)/shard_map/conv/pallas_call | solution.py:79
  257.2 5.8 %collective-permute-done.36.refs_2_ = bf16[512,768]{1,0:T(8,128)(2,1)S(1)} collective-permute-done((bf16[512,768]{1,0:T(8,128)(2,1)S(1)}, bf16[512,768]{1,0:T(8,128)(2,1)S(1)}, u32[]{:S(2)}, u32[]{:S(2)}) %collective-permute-start.36) | collective-permute-done | bytes 786464 | tf_op jit(solution)/shard_map/ppermute | solution.py:459
  268.0 12.0 %collective-permute-done.38.refs_2_ = bf16[512,768]{1,0:T(8,128)(2,1)S(1)} collective-permute-done((bf16[512,768]{1,0:T(8,128)(2,1)S(1)}, bf16[512,768]{1,0:T(8,128)(2,1)S(1)}, u32[]{:S(2)}, u32[]{:S(2)}) %collective-permute-start.38) | collective-permute-done | bytes 786464 | tf_op jit(solution)/shard_map/ppermute | solution.py:459
  281.5 4.6 %collective-permute-start.41 = (bf16[8,128,256]{2,1,0:T(8,128)(2,1)S(1)}, bf16[8,128,256]{2,1,0:T(8,128)(2,1)S(1)}, u32[]{:S(2)}, u32[]{:S(2)}) collective-permute-start(bf16[8,128,256]{2,1,0:T(8,128)(2,1)S(1)} %get-tuple-element.168), channel_id=1, source_target_pairs={{0,8},{1,9},{2,10},{3,11},{4,12},{5,13},{6,14},{7,15}} | collective-permute-start | bytes 1572872 | tf_op jit(solution)/shard_map/ppermute | solution.py:468
  286.9 5.9 %conv.6 = (bf16[8,128,256]{2,1,0:T(8,128)(2,1)S(1)}, f32[16,256]{1,0:T(8,128)S(1)}, f32[8,768]{1,0:T(8,128)S(1)}) custom-call(s32[8]{0:T(128)S(1)} %get-tuple-element.220.order, s32[8]{0:T(128)S(1)} %get-tuple-element.216.pick, f32[4,128,768]{2,1,0:T(8,128)S(1)} %bitcast.35, f32[4,128,768]{2,1,0:T(8,128)S(1)} %bitcast.36, f32[3,768]{1,0:T(4,128)S(1)} %bitcast.39, ...), custom_call_target="tpu_custom_call" | custom-call | tf_op jit(solution)/shard_map/conv/pallas_call | solution.py:79
  297.8 15.6 %collective-permute-done.44.refs_1_ = bf16[512,768]{1,0:T(8,128)(2,1)S(1)} collective-permute-done((bf16[512,768]{1,0:T(8,128)(2,1)S(1)}, bf16[512,768]{1,0:T(8,128)(2,1)S(1)}, u32[]{:S(2)}, u32[]{:S(2)}) %collective-permute-start.44) | collective-permute-done | bytes 786464 | tf_op jit(solution)/shard_map/ppermute | solution.py:459
  317.2 6.4 %conv.7 = (bf16[8,128,256]{2,1,0:T(8,128)(2,1)S(1)}, f32[16,256]{1,0:T(8,128)}, f32[8,768]{1,0:T(8,128)}) custom-call(s32[8]{0:T(128)S(1)} %get-tuple-element.223.order, s32[8]{0:T(128)S(1)} %get-tuple-element.195.pick, f32[4,128,768]{2,1,0:T(8,128)S(1)} %bitcast.28, f32[4,128,768]{2,1,0:T(8,128)S(1)} %bitcast.29, f32[3,768]{1,0:T(4,128)S(1)} %bitcast.40, ...), custom_call_target="tpu_custom_call" | custom-call | tf_op jit(solution)/shard_map/conv/pallas_call | solution.py:79
  323.6 7.3 %collective-permute-start.48 = (bf16[8,128,256]{2,1,0:T(8,128)(2,1)S(1)}, bf16[8,128,256]{2,1,0:T(8,128)(2,1)}, u32[]{:S(2)}, u32[]{:S(2)}) collective-permute-start(bf16[8,128,256]{2,1,0:T(8,128)(2,1)S(1)} %get-tuple-element.192), channel_id=1, source_target_pairs={{0,24},{1,25},{2,26},{3,27},{4,28},{5,29},{6,30},{7,31}} | collective-permute-start | bytes 1572872 | tf_op jit(solution)/shard_map/ppermute | solution.py:479
  345.5 11.4 %all_to_all.15.second = bf16[8,128,256]{2,1,0:T(8,128)(2,1)S(1)} all-to-all(bf16[8,128,256]{2,1,0:T(8,128)(2,1)S(1)} %add_add_fusion), channel_id=1, replica_groups=mesh['z'=4,'x'=2,'y'=2,'c'=2] {'x','y','c'}, dimensions={0} | all-to-all | bytes 1048576 | tf_op jit(solution)/shard_map/all_to_all | solution.py:484
  (179 shorter events, 155.5 us)
Async XLA Ops:
  3.0 56.4 %all-to-all-start = ((bf16[4,128,2048]{2,1,0:T(8,128)(2,1)}), bf16[4,128,2048]{2,1,0:T(8,128)(2,1)}, u32[]{:S(2)}, u32[]{:S(2)}) async-start(bf16[4,128,2048]{2,1,0:T(8,128)(2,1)} %cut_tokens.1), calls=%async_computation | async-start | bytes 4194304 | tf_op jit(solution)/shard_map/all_to_all | solution.py:323
  10.8 36.0 %collective-permute-start = (bf16[1024,768]{1,0:T(8,128)(2,1)S(1)}, bf16[1024,768]{1,0:T(8,128)(2,1)}, u32[]{:S(2)}, u32[]{:S(2)}) collective-permute-start(bf16[1024,768]{1,0:T(8,128)(2,1)S(1)} %cut_weight.5), channel_id=1, source_target_pairs={{0,4},{4,0},{1,5},{5,1},{2,6},{6,2},{3,7},{7,3},{8,12},{12,8},{9,1... | collective-permute-start | bytes 4718600 | tf_op jit(solution)/shard_map/ppermute | solution.py:307
  79.8 31.2 %collective-permute-start.14 = (bf16[128,2048]{1,0:T(8,128)(2,1)S(1)}, bf16[128,2048]{1,0:T(8,128)(2,1)S(1)}, u32[]{:S(2)}, u32[]{:S(2)}) collective-permute-start(bf16[128,2048]{1,0:T(8,128)(2,1)S(1)} %get-tuple-element.118), channel_id=1, source_target_pairs={{0,4},{4,0},{1,5},{5,1},{2,6},{6,2},{3,7},{7,3},{8,12},{12,8},{9,1... | collective-permute-start | bytes 1572872 | tf_op jit(solution)/shard_map/ppermute | solution.py:284
  81.3 33.5 %collective-permute-start.8 = (bf16[512,768]{1,0:T(8,128)(2,1)S(1)}, bf16[512,768]{1,0:T(8,128)(2,1)S(1)}, u32[]{:S(2)}, u32[]{:S(2)}) collective-permute-start(bf16[512,768]{1,0:T(8,128)(2,1)S(1)} %chain.28), channel_id=1, source_target_pairs={{0,8},{1,9},{2,10},{3,11},{4,12},{5,13},{6,14},{7,15}} | collective-permute-start | bytes 2359304 | tf_op jit(solution)/shard_map/ppermute | solution.py:454
  141.5 31.3 %collective-permute-start.27 = (bf16[256,2048]{1,0:T(8,128)(2,1)S(1)}, bf16[256,2048]{1,0:T(8,128)(2,1)S(1)}, u32[]{:S(2)}, u32[]{:S(2)}) collective-permute-start(bf16[256,2048]{1,0:T(8,128)(2,1)S(1)} %constant_dynamic-update-slice_fusion.2.refs_0_), channel_id=1, source_target_pairs={{0,4},{4,0},{1,5},{5,1},{2,6},{6,2},{3,7},{7,3},{8,12},{12,8},{9,1... | collective-permute-start | bytes 3145736 | tf_op jit(solution)/shard_map/ppermute | solution.py:374
  143.7 28.8 %collective-permute-start.21 = (bf16[512,768]{1,0:T(8,128)(2,1)S(1)}, bf16[512,768]{1,0:T(8,128)(2,1)S(1)}, u32[]{:S(2)}, u32[]{:S(2)}) collective-permute-start(bf16[512,768]{1,0:T(8,128)(2,1)S(1)} %chain.34), channel_id=1, source_target_pairs={{0,8},{8,16},{1,9},{9,17},{2,10},{10,18},{3,11},{11,19},{4,12},{12... | collective-permute-start | bytes 2359304 | tf_op jit(solution)/shard_map/ppermute | solution.py:454
  156.0 26.4 %collective-permute-start.24 = (bf16[256,2048]{1,0:T(8,128)(2,1)S(1)}, bf16[256,2048]{1,0:T(8,128)(2,1)S(1)}, u32[]{:S(2)}, u32[]{:S(2)}) collective-permute-start(bf16[256,2048]{1,0:T(8,128)(2,1)S(1)} %constant_dynamic-update-slice_fusion.2.refs_0_), channel_id=1, source_target_pairs={{0,1},{1,0},{2,3},{3,2},{4,5},{5,4},{6,7},{7,6},{8,9},{9,8},{10,11... | collective-permute-start | bytes 3145736 | tf_op jit(solution)/shard_map/ppermute | solution.py:416
  156.8 32.5 %collective-permute-start.25 = (bf16[512,768]{1,0:T(8,128)(2,1)S(1)}, bf16[512,768]{1,0:T(8,128)(2,1)S(1)}, u32[]{:S(2)}, u32[]{:S(2)}) collective-permute-start(bf16[512,768]{1,0:T(8,128)(2,1)S(1)} %chain.36), channel_id=1, source_target_pairs={{0,8},{8,16},{16,24},{1,9},{9,17},{17,25},{2,10},{10,18},{18,26},{... | collective-permute-start | bytes 2359304 | tf_op jit(solution)/shard_map/ppermute | solution.py:454
  172.8 27.0 %collective-permute-start.28 = (bf16[256,2048]{1,0:T(8,128)(2,1)S(1)}, bf16[256,2048]{1,0:T(8,128)(2,1)S(1)}, u32[]{:S(2)}, u32[]{:S(2)}) collective-permute-start(bf16[256,2048]{1,0:T(8,128)(2,1)S(1)} %collective-permute-done.27.refs_0_), channel_id=1, source_target_pairs={{0,1},{1,0},{2,3},{3,2},{4,5},{5,4},{6,7},{7,6},{8,9},{9,8},{10,11... | collective-permute-start | bytes 3145736 | tf_op jit(solution)/shard_map/ppermute | solution.py:416
  174.2 32.0 %collective-permute-start.29 = (bf16[512,768]{1,0:T(8,128)(2,1)S(1)}, bf16[512,768]{1,0:T(8,128)(2,1)S(1)}, u32[]{:S(2)}, u32[]{:S(2)}) collective-permute-start(bf16[512,768]{1,0:T(8,128)(2,1)S(1)} %chain.38), channel_id=1, source_target_pairs={{0,8},{8,16},{16,24},{1,9},{9,17},{17,25},{2,10},{10,18},{18,26},{... | collective-permute-start | bytes 2359304 | tf_op jit(solution)/shard_map/ppermute | solution.py:454
  182.3 30.2 %collective-permute-start.30 = (bf16[512,768]{1,0:T(8,128)(2,1)S(1)}, bf16[512,768]{1,0:T(8,128)(2,1)S(1)}, u32[]{:S(2)}, u32[]{:S(2)}) collective-permute-start(bf16[512,768]{1,0:T(8,128)(2,1)S(1)} %chain.39), channel_id=1, source_target_pairs={{24,16},{16,8},{8,0},{25,17},{17,9},{9,1},{26,18},{18,10},{10,2},{... | collective-permute-start | bytes 2359304 | tf_op jit(solution)/shard_map/ppermute | solution.py:459
  189.7 33.3 %collective-permute-start.31 = (bf16[512,768]{1,0:T(8,128)(2,1)S(1)}, bf16[512,768]{1,0:T(8,128)(2,1)S(1)}, u32[]{:S(2)}, u32[]{:S(2)}) collective-permute-start(bf16[512,768]{1,0:T(8,128)(2,1)S(1)} %get-tuple-element.136), channel_id=1, source_target_pairs={{0,8},{8,16},{16,24},{1,9},{9,17},{17,25},{2,10},{10,18},{18,26},{... | collective-permute-start | bytes 2359304 | tf_op jit(solution)/shard_map/ppermute | solution.py:454
  196.0 33.4 %collective-permute-start.32 = (bf16[512,768]{1,0:T(8,128)(2,1)S(1)}, bf16[512,768]{1,0:T(8,128)(2,1)S(1)}, u32[]{:S(2)}, u32[]{:S(2)}) collective-permute-start(bf16[512,768]{1,0:T(8,128)(2,1)S(1)} %get-tuple-element.139), channel_id=1, source_target_pairs={{24,16},{16,8},{8,0},{25,17},{17,9},{9,1},{26,18},{18,10},{10,2},{... | collective-permute-start | bytes 2359304 | tf_op jit(solution)/shard_map/ppermute | solution.py:459
  206.5 33.1 %collective-permute-start.33 = (bf16[512,768]{1,0:T(8,128)(2,1)S(1)}, bf16[512,768]{1,0:T(8,128)(2,1)S(1)}, u32[]{:S(2)}, u32[]{:S(2)}) collective-permute-start(bf16[512,768]{1,0:T(8,128)(2,1)S(1)} %get-tuple-element.145), channel_id=1, source_target_pairs={{0,8},{8,16},{16,24},{1,9},{9,17},{17,25},{2,10},{10,18},{18,26},{... | collective-permute-start | bytes 2359304 | tf_op jit(solution)/shard_map/ppermute | solution.py:454
  212.8 33.4 %collective-permute-start.34 = (bf16[512,768]{1,0:T(8,128)(2,1)S(1)}, bf16[512,768]{1,0:T(8,128)(2,1)S(1)}, u32[]{:S(2)}, u32[]{:S(2)}) collective-permute-start(bf16[512,768]{1,0:T(8,128)(2,1)S(1)} %get-tuple-element.148), channel_id=1, source_target_pairs={{24,16},{16,8},{8,0},{25,17},{17,9},{9,1},{26,18},{18,10},{10,2},{... | collective-permute-start | bytes 2359304 | tf_op jit(solution)/shard_map/ppermute | solution.py:459
  223.0 33.4 %collective-permute-start.35 = (bf16[512,768]{1,0:T(8,128)(2,1)S(1)}, bf16[512,768]{1,0:T(8,128)(2,1)S(1)}, u32[]{:S(2)}, u32[]{:S(2)}) collective-permute-start(bf16[512,768]{1,0:T(8,128)(2,1)S(1)} %get-tuple-element.151), channel_id=1, source_target_pairs={{8,16},{16,24},{9,17},{17,25},{10,18},{18,26},{11,19},{19,27},{12,... | collective-permute-start | bytes 2359304 | tf_op jit(solution)/shard_map/ppermute | solution.py:454
  229.7 33.4 %collective-permute-start.36 = (bf16[512,768]{1,0:T(8,128)(2,1)S(1)}, bf16[512,768]{1,0:T(8,128)(2,1)S(1)}, u32[]{:S(2)}, u32[]{:S(2)}) collective-permute-start(bf16[512,768]{1,0:T(8,128)(2,1)S(1)} %get-tuple-element.154), channel_id=1, source_target_pairs={{16,8},{8,0},{17,9},{9,1},{18,10},{10,2},{19,11},{11,3},{20,12},{1... | collective-permute-start | bytes 2359304 | tf_op jit(solution)/shard_map/ppermute | solution.py:459
  239.6 27.6 %collective-permute-start.37 = (bf16[512,768]{1,0:T(8,128)(2,1)S(1)}, bf16[512,768]{1,0:T(8,128)(2,1)S(1)}, u32[]{:S(2)}, u32[]{:S(2)}) collective-permute-start(bf16[512,768]{1,0:T(8,128)(2,1)S(1)} %get-tuple-element.161), channel_id=1, source_target_pairs={{8,16},{16,24},{9,17},{17,25},{10,18},{18,26},{11,19},{19,27},{12,... | collective-permute-start | bytes 2359304 | tf_op jit(solution)/shard_map/ppermute | solution.py:454
  246.5 33.4 %collective-permute-start.38 = (bf16[512,768]{1,0:T(8,128)(2,1)S(1)}, bf16[512,768]{1,0:T(8,128)(2,1)S(1)}, u32[]{:S(2)}, u32[]{:S(2)}) collective-permute-start(bf16[512,768]{1,0:T(8,128)(2,1)S(1)} %get-tuple-element.164), channel_id=1, source_target_pairs={{16,8},{8,0},{17,9},{9,1},{18,10},{10,2},{19,11},{11,3},{20,12},{1... | collective-permute-start | bytes 2359304 | tf_op jit(solution)/shard_map/ppermute | solution.py:459
  256.5 29.7 %collective-permute-start.39 = (bf16[512,768]{1,0:T(8,128)(2,1)S(1)}, bf16[512,768]{1,0:T(8,128)(2,1)S(1)}, u32[]{:S(2)}, u32[]{:S(2)}) collective-permute-start(bf16[512,768]{1,0:T(8,128)(2,1)S(1)} %get-tuple-element.171), channel_id=1, source_target_pairs={{16,24},{17,25},{18,26},{19,27},{20,28},{21,29},{22,30},{23,31}} | collective-permute-start | bytes 2359304 | tf_op jit(solution)/shard_map/ppermute | solution.py:454
  263.4 33.4 %collective-permute-start.40 = (bf16[512,768]{1,0:T(8,128)(2,1)S(1)}, bf16[512,768]{1,0:T(8,128)(2,1)S(1)}, u32[]{:S(2)}, u32[]{:S(2)}) collective-permute-start(bf16[512,768]{1,0:T(8,128)(2,1)S(1)} %get-tuple-element.174), channel_id=1, source_target_pairs={{8,0},{9,1},{10,2},{11,3},{12,4},{13,5},{14,6},{15,7}} | collective-permute-start | bytes 2359304 | tf_op jit(solution)/shard_map/ppermute | solution.py:459
  267.2 30.6 %collective-permute-start.43 = (bf16[512,768]{1,0:T(8,128)(2,1)S(1)}, bf16[512,768]{1,0:T(8,128)(2,1)S(1)}, u32[]{:S(2)}, u32[]{:S(2)}) collective-permute-start(bf16[512,768]{1,0:T(8,128)(2,1)S(1)} %get-tuple-element.177), channel_id=1, source_target_pairs={{16,24},{17,25},{18,26},{19,27},{20,28},{21,29},{22,30},{23,31}} | collective-permute-start | bytes 2359304 | tf_op jit(solution)/shard_map/ppermute | solution.py:454
  280.2 33.2 %collective-permute-start.44 = (bf16[512,768]{1,0:T(8,128)(2,1)S(1)}, bf16[512,768]{1,0:T(8,128)(2,1)S(1)}, u32[]{:S(2)}, u32[]{:S(2)}) collective-permute-start(bf16[512,768]{1,0:T(8,128)(2,1)S(1)} %get-tuple-element.180), channel_id=1, source_target_pairs={{8,0},{9,1},{10,2},{11,3},{12,4},{13,5},{14,6},{15,7}} | collective-permute-start | bytes 2359304 | tf_op jit(solution)/shard_map/ppermute | solution.py:459
  296.8 34.1 %collective-permute-start.46 = (bf16[8,128,256]{2,1,0:T(8,128)(2,1)S(1)}, bf16[8,128,256]{2,1,0:T(8,128)(2,1)S(1)}, u32[]{:S(2)}, u32[]{:S(2)}) collective-permute-start(bf16[8,128,256]{2,1,0:T(8,128)(2,1)S(1)} %get-tuple-element.185), channel_id=1, source_target_pairs={{24,16},{25,17},{26,18},{27,19},{28,20},{29,21},{30,22},{31,23}} | collective-permute-start | bytes 1572872 | tf_op jit(solution)/shard_map/ppermute | solution.py:479
  (35 other events, 582.5 us)
